TPU v7x, 512 devices: a whole 4x8x8 slice. The times are simulated.
512 devices in a mesh: dp: 32 (over z_lo, y, core), tensor: 16 (over z_hi, x).
Axes of the slice: x: 4, y: 8, z: 8 (z_hi: 4, z_lo: 2; z = z_hi * 2 + z_lo), core: 2. Of those that a mesh axis runs over, the one named last changes fastest.
Arguments:
- inputs: bfloat16 [1024, 2560], P(('dp', 'tensor')), may hold values from -6 to 6
- curvature: float32 [1024], P(('dp', 'tensor')), may hold values from 0.25 to 4
- w_gate: bfloat16 [2560, 13824], P('dp', 'tensor'), may hold values from -0.125 to 0.125
- w_up: bfloat16 [2560, 13824], P('dp', 'tensor'), may hold values from -0.125 to 0.125
- w_down: bfloat16 [13824, 2560], P('tensor', 'dp'), may hold values from -0.0546875 to 0.0546875
- v_gate: bfloat16 [2560, 13824], P('dp', 'tensor'), may hold values from -0.125 to 0.125
- v_up: bfloat16 [2560, 13824], P('dp', 'tensor'), may hold values from -0.125 to 0.125
- v_down: bfloat16 [13824, 2560], P('tensor', 'dp'), may hold values from -0.0546875 to 0.0546875
Outputs:
- tangent_out: bfloat16 [1024, 2560], P(('dp', 'tensor'))
- prod_gate: float32 [2560, 13824], P('dp', 'tensor')
- prod_up: float32 [2560, 13824], P('dp', 'tensor')
- prod_down: float32 [13824, 2560], P('tensor', 'dp')
All inputs are finite; a program needn't handle non-finite values.
Results may differ from a plain program's by a relative error of at most 0.024.
Values may be sent and summed in bfloat16 or wider, within the bound.
A program may use at most 128 MiB of HBM per device.

v0:
```python
import jax
import jax.numpy as jnp
from jax import lax
from jax.sharding import PartitionSpec as P


def contract_rows(left, right):
    return lax.dot_general(
        left, right, (((0,), (0,)), ((), ())), preferred_element_type=jnp.float32
    )


def contract_cols(left, right):
    return lax.dot_general(
        left, right, (((1,), (1,)), ((), ())), preferred_element_type=jnp.float32
    )


def on_device(inputs, curvature, w_gate, w_up, w_down, v_gate, v_up, v_down):
    rows, curv_all = (
        lax.all_gather(inputs, "tensor", axis=0, tiled=True),
        lax.all_gather(curvature.astype(jnp.bfloat16), "tensor", axis=0, tiled=True).astype(
            curvature.dtype
        ),
    )
    pieces = (
        lax.all_gather(w_gate, "dp", axis=0, tiled=True),
        lax.all_gather(w_up, "dp", axis=0, tiled=True),
        lax.all_gather(v_gate, "dp", axis=0, tiled=True),
        lax.all_gather(v_up, "dp", axis=0, tiled=True),
    )
    cols = rows
    gate, up, dgate, dup = tuple(
        (jnp.dot(cols, p, preferred_element_type=jnp.float32) for p in pieces)
    )
    sig = jax.nn.sigmoid(gate)
    act = gate * sig
    slope = sig * (1.0 + gate * (1.0 - sig))
    hidden = (act * up).astype(jnp.bfloat16)
    thidden = (slope * dgate * up + act * dup).astype(jnp.bfloat16)
    pieces = lax.all_gather((w_down, v_down), "dp", axis=1, tiled=True)
    terms = jnp.dot(thidden, pieces[0], preferred_element_type=jnp.float32) + jnp.dot(
        hidden, pieces[1], preferred_element_type=jnp.float32
    )
    tangent = lax.psum_scatter(
        terms.astype(jnp.bfloat16), "tensor", scatter_dimension=0, tiled=True
    ).astype(jnp.float32)
    weighted = (curvature[:, None] * tangent).astype(jnp.bfloat16)
    weighted_all = lax.all_gather(weighted, "tensor", axis=0, tiled=True)
    tangent_out = tangent.astype(jnp.bfloat16)
    cols = weighted_all
    dhid = contract_cols(cols, lax.all_gather(w_down, "dp", axis=1, tiled=True))
    bgate = (dhid * up * slope).astype(jnp.bfloat16)
    bup = (dhid * act).astype(jnp.bfloat16)
    mine_rows, mine_weighted = (
        lax.all_to_all(rows, "dp", split_axis=1, concat_axis=0, tiled=True),
        lax.all_to_all(weighted_all, "dp", split_axis=1, concat_axis=0, tiled=True),
    )
    pieces = (
        lax.all_gather(bgate, "dp", axis=0, tiled=True),
        lax.all_gather(bup, "dp", axis=0, tiled=True),
        lax.all_gather(hidden, "dp", axis=0, tiled=True),
    )
    prod_gate = contract_rows(mine_rows, pieces[0])
    prod_up = contract_rows(mine_rows, pieces[1])
    prod_down = contract_rows(pieces[2], mine_weighted)
    return (tangent_out, prod_gate, prod_up, prod_down)


def solution(mesh):
    return jax.shard_map(
        on_device,
        mesh=mesh,
        in_specs=(
            P(("dp", "tensor"), None),
            P(("dp", "tensor")),
            P("dp", "tensor"),
            P("dp", "tensor"),
            P("tensor", "dp"),
            P("dp", "tensor"),
            P("dp", "tensor"),
            P("tensor", "dp"),
        ),
        out_specs=(
            P(("dp", "tensor"), None),
            P("dp", "tensor"),
            P("dp", "tensor"),
            P("tensor", "dp"),
        ),
        check_vma=False,
    )
```

profile of v0, /device:TPU:1, one launch (start us, length us, event | category | flops | bytes accessed | tf_op | source)
XLA Modules:
  0.0 826.1 jit_solution(17743783934637923280)
XLA Ops:
  11.2 44.6 %all-gather = bf16[16,2,2560]{2,1,0:T(2,128)(2,1)S(1)} all-gather(bf16[1,2,2560]{2,1,0:T(2,128)(2,1)} %bitcast.36), channel_id=1, replica_groups=mesh['dp'=32,'tensor'=16] {'tensor'}, dimensions={0}, use_global_device_ids=true | all-gather | bytes 174080 | tf_op jit(solution)/shard_map/all_gather | solution.py:21
  55.8 30.2 %all-gather.12.cloned.1.call-done = bf16[2560,864]{1,0:T(8,128)(2,1)} async-done(((bf16[80,864]{1,0:T(8,128)(2,1)}), bf16[2560,864]{1,0:T(8,128)(2,1)}) %all-gather.12.cloned.1.call-update) | async-done | bytes 4423696 | tf_op jit(solution)/shard_map/all_gather | solution.py:27
  86.0 3.1 fusion.8
  89.1 69.0 %all-gather.16.cloned.1.call-done = bf16[2560,864]{1,0:T(8,128)(2,1)} async-done(((bf16[80,864]{1,0:T(8,128)(2,1)}), bf16[2560,864]{1,0:T(8,128)(2,1)}) %all-gather.16.cloned.1.call-update) | async-done | bytes 4423696 | tf_op jit(solution)/shard_map/all_gather | solution.py:28
  158.1 3.2 multiply_convert_fusion.2
  161.3 68.6 %all-gather.14.cloned.1.call-done = bf16[2560,864]{1,0:T(8,128)(2,1)} async-done(((bf16[80,864]{1,0:T(8,128)(2,1)}), bf16[2560,864]{1,0:T(8,128)(2,1)}) %all-gather.14.cloned.1.call-update) | async-done | bytes 4423696 | tf_op jit(solution)/shard_map/all_gather | solution.py:29
  229.9 3.2 fusion.2
  233.0 68.4 %all-gather.20.cloned.1.call-done = bf16[864,2560]{0,1:T(8,128)(2,1)} async-done(((bf16[864,80]{0,1:T(8,128)(2,1)}), bf16[864,2560]{0,1:T(8,128)(2,1)}) %all-gather.20.cloned.1.call-update) | async-done | bytes 4423696 | tf_op jit(solution)/shard_map/all_gather | solution.py:41
  301.4 71.6 %all-gather.18.cloned.1.call-done = bf16[2560,864]{1,0:T(8,128)(2,1)} async-done(((bf16[80,864]{1,0:T(8,128)(2,1)}), bf16[2560,864]{1,0:T(8,128)(2,1)}) %all-gather.18.cloned.1.call-update) | async-done | bytes 4423696 | tf_op jit(solution)/shard_map/all_gather | solution.py:30
  373.0 5.8 fusion.4
  378.8 65.8 %all-gather.22.cloned.1.call-done = bf16[864,2560]{0,1:T(8,128)(2,1)} async-done(((bf16[864,80]{0,1:T(8,128)(2,1)}), bf16[864,2560]{0,1:T(8,128)(2,1)}) %all-gather.22.cloned.1.call-update) | async-done | bytes 4423696 | tf_op jit(solution)/shard_map/all_gather | solution.py:41
  444.5 4.4 fusion
  451.7 147.7 %all-reduce.3.cloned.1.call-done = bf16[32,2560]{1,0:T(8,128)(2,1)} async-done(((bf16[32,2560]{1,0:T(8,128)(2,1)}), bf16[32,2560]{1,0:T(8,128)(2,1)}) %all-reduce.3.cloned.1.call-update) | async-done | bytes 163856
  600.8 36.5 %all-gather.1 = bf16[16,2,2560]{2,1,0:T(2,128)(2,1)S(1)} all-gather(bf16[1,2,2560]{2,1,0:T(2,128)(2,1)S(1)} %get-tuple-element.4), channel_id=1, replica_groups=mesh['dp'=32,'tensor'=16] {'tensor'}, dimensions={0}, use_global_device_ids=true | all-gather | bytes 174080 | tf_op jit(solution)/shard_map/all_gather | solution.py:49
  637.4 3.8 multiply_convert_fusion
  642.9 21.8 %all-to-all-start.1 = ((bf16[32,32,80]{2,0,1:T(8,128)(2,1)}), bf16[32,32,80]{2,0,1:T(8,128)(2,1)S(1)}, u32[]{:S(2)}, u32[]{:S(2)}) async-start(bf16[32,32,80]{2,0,1:T(8,128)(2,1)} %copy.15), calls=%async_computation.1 | async-start | bytes 524288 | tf_op jit(solution)/shard_map/all_to_all | solution.py:57
  665.8 11.1 %all-to-all-done.1 = bf16[32,32,80]{2,0,1:T(8,128)(2,1)S(1)} async-done(((bf16[32,32,80]{2,0,1:T(8,128)(2,1)}), bf16[32,32,80]{2,0,1:T(8,128)(2,1)S(1)}, u32[]{:S(2)}, u32[]{:S(2)}) %all-to-all-start.1) | async-done | bytes 163872 | tf_op jit(solution)/shard_map/all_to_all | solution.py:57
  677.0 5.2 all-to-all-start
  682.2 2.7 fusion.9
  684.9 9.3 %all-to-all-done = bf16[32,32,80]{2,0,1:T(8,128)(2,1)S(1)} async-done(((bf16[32,32,80]{2,0,1:T(8,128)(2,1)}), bf16[32,32,80]{2,0,1:T(8,128)(2,1)S(1)}, u32[]{:S(2)}, u32[]{:S(2)}) %all-to-all-start) | async-done | bytes 163872 | tf_op jit(solution)/shard_map/all_to_all | solution.py:56
  694.2 53.2 %all-gather.26.cloned.1.call-done = bf16[1024,864]{1,0:T(8,128)(2,1)} async-done(((bf16[32,864]{1,0:T(8,128)(2,1)}), bf16[1024,864]{1,0:T(8,128)(2,1)}) %all-gather.26.cloned.1.call-update) | async-done | bytes 1769488 | tf_op jit(solution)/shard_map/all_gather | solution.py:61
  747.4 2.7 convolution_bitcast_fusion
  750.1 66.5 %all-gather.24.cloned.1.call-done = bf16[1024,864]{1,0:T(8,128)(2,1)} async-done(((bf16[32,864]{1,0:T(8,128)(2,1)}), bf16[1024,864]{1,0:T(8,128)(2,1)}) %all-gather.24.cloned.1.call-update) | async-done | bytes 1769488 | tf_op jit(solution)/shard_map/all_gather | solution.py:60
  816.6 2.7 convolution_bitcast_fusion.1
  (33 shorter events, 10.3 us)
Async XLA Ops:
  7.2 78.8 %all-gather.12.cloned.1.call-start = ((), (), s32[]{:S(2)}) async-start(), calls=%async_computation.2 | async-start | bytes 4730880 | tf_op jit(solution)/shard_map/all_gather | solution.py:27
  7.9 150.2 %all-gather.16.cloned.1.call-start = ((), (), s32[]{:S(2)}) async-start(), calls=%async_computation.4 | async-start | bytes 4730880 | tf_op jit(solution)/shard_map/all_gather | solution.py:28
  8.6 221.2 %all-gather.14.cloned.1.call-start = ((), (), s32[]{:S(2)}) async-start(), calls=%async_computation.3 | async-start | bytes 4730880 | tf_op jit(solution)/shard_map/all_gather | solution.py:29
  9.4 292.0 %all-gather.20.cloned.1.call-start = ((), (), s32[]{:S(2)}) async-start(), calls=%async_computation.6 | async-start | bytes 4730880 | tf_op jit(solution)/shard_map/all_gather | solution.py:41
  10.0 363.0 %all-gather.18.cloned.1.call-start = ((), (), s32[]{:S(2)}) async-start(), calls=%async_computation.5 | async-start | bytes 4730880 | tf_op jit(solution)/shard_map/all_gather | solution.py:30
  10.5 434.0 %all-gather.22.cloned.1.call-start = ((), (), s32[]{:S(2)}) async-start(), calls=%async_computation.7 | async-start | bytes 4730880 | tf_op jit(solution)/shard_map/all_gather | solution.py:41
  11.1 588.3 %all-reduce.3.cloned.1.call-start = ((), (), s32[]{:S(2)}) async-start(), calls=%async_computation.11 | async-start | bytes 327680
  161.3 283.3 %copy-start = (bf16[32,864]{1,0:T(8,128)(2,1)}, bf16[32,864]{1,0:T(8,128)(2,1)S(1)}, u32[]{:S(2)}) copy-start(bf16[32,864]{1,0:T(8,128)(2,1)S(1)} %get-tuple-element.8) | copy-start | bytes 165892
  378.8 220.7 %copy-start.1 = (f32[2]{0:T(128)S(1)}, f32[2]{0:T(128)}, u32[]{:S(2)}) copy-start(f32[2]{0:T(128)} %param.9) | copy-start | bytes 28
  449.0 233.3 %all-gather.28.cloned.1.call-start = ((), (), s32[]{:S(2)}) async-start(), calls=%async_computation.10 | async-start | bytes 1892352 | tf_op jit(solution)/shard_map/all_gather | solution.py:62
  449.7 297.7 %all-gather.26.cloned.1.call-start = ((), (), s32[]{:S(2)}) async-start(), calls=%async_computation.9 | async-start | bytes 1892352 | tf_op jit(solution)/shard_map/all_gather | solution.py:61
  641.2 175.4 %all-gather.24.cloned.1.call-start = ((), (), s32[]{:S(2)}) async-start(), calls=%async_computation.8 | async-start | bytes 1892352 | tf_op jit(solution)/shard_map/all_gather | solution.py:60
  642.9 34.1 %all-to-all-start.1 = ((bf16[32,32,80]{2,0,1:T(8,128)(2,1)}), bf16[32,32,80]{2,0,1:T(8,128)(2,1)S(1)}, u32[]{:S(2)}, u32[]{:S(2)}) async-start(bf16[32,32,80]{2,0,1:T(8,128)(2,1)} %copy.15), calls=%async_computation.1 | async-start | bytes 524288 | tf_op jit(solution)/shard_map/all_to_all | solution.py:57
  677.0 17.3 %all-to-all-start = ((bf16[32,32,80]{2,0,1:T(8,128)(2,1)}), bf16[32,32,80]{2,0,1:T(8,128)(2,1)S(1)}, u32[]{:S(2)}, u32[]{:S(2)}) async-start(bf16[32,32,80]{2,0,1:T(8,128)(2,1)} %copy.14), calls=%async_computation | async-start | bytes 524288 | tf_op jit(solution)/shard_map/all_to_all | solution.py:56
Sparse Core Ops, SparseCore 0:
  10.1 75.7 all-gather.11
  88.1 69.9 all-gather.15
  160.3 69.5 all-gather.13
  231.9 69.5 all-gather.19
  303.4 69.5 all-gather.17
  375.0 69.5 all-gather.21
  449.1 150.2 all-reduce.2
  601.8 75.7 all-gather.27
  680.5 66.8 all-gather.25
  749.6 66.8 all-gather.23
where the time goes:
time: 827 us; the launch traced here: 826 us
  waiting for transfers between devices  666 us (81%)
  blocking collectives  81 us (10%)
  matrix products  31.5 us (4%)
  starting transfers between devices  27.4 us (3%)
  between operations  14.9 us (2%)
    unnamed x11, waiting for transfers between devices  153 us
    all_gather x2, waiting for transfers between devices, on_device(): pieces = lax.all_gather((w_down, v_down), 'dp', axis=1, tiled=True)  134 us
    all_gather x1, waiting for transfers between devices, on_device(): lax.all_gather(v_up, 'dp', axis=0, tiled=True)  71.6 us
    all_gather x1, waiting for transfers between devices, on_device(): lax.all_gather(w_up, 'dp', axis=0, tiled=True)  69 us
    all_gather x1, waiting for transfers between devices, on_device(): lax.all_gather(v_gate, 'dp', axis=0, tiled=True)  68.6 us
    all_gather x1, waiting for transfers between devices, on_device(): lax.all_gather(bgate, 'dp', axis=0, tiled=True)  66.5 us
    all_gather x1, waiting for transfers between devices, on_device(): lax.all_gather(bup, 'dp', axis=0, tiled=True)  53.2 us
    all_gather x1, blocking collectives, on_device(): lax.all_gather(inputs, 'tensor', axis=0, tiled=True)  44.6 us
  transfers between devices with their start and end apart: 12, of which 11 were waited for; matrix products, arithmetic and copies ran while one was open for 3% of the time, Pallas kernels for 0%

commit v1 on v0

v1 whole, which is shorter than its diff:
```python
import functools

import jax
import jax.numpy as jnp
from jax import lax
from jax.experimental import pallas as pl
from jax.experimental.pallas import tpu as pltpu
from jax.sharding import PartitionSpec as P

MESH = pl.DeviceIdType.MESH
BF = jnp.bfloat16
F32 = jnp.float32


def dot(a, b, ca, cb):
    return lax.dot_general(a, b, (((ca,), (cb,)), ((), ())), preferred_element_type=F32)


class Link:
    def __init__(self, sems, slot, src, dst, device):
        self.copy = pltpu.make_async_remote_copy(
            src_ref=src,
            dst_ref=dst,
            send_sem=sems[0].at[slot],
            recv_sem=sems[1].at[slot],
            device_id=device,
            device_id_type=MESH,
        )
        self.copy.start()

    def arrive(self):
        self.copy.wait_recv()

    def left(self):
        self.copy.wait_send()


def kernel(
    NY, NT, D, F, KP,
    xs, wg, wu, vg, vu, wd, vd,
    to, pg, pu, pd,
    stage, xin, X, W, Pf, Pd, rs_s, rs_r, dh_s, dh_r, H, B,
    Tf, Tb, trecv, wt, osend, orecv, PF, PB, C1, zs, zr,
    send_sems, recv_sems, local_sems,
):
    K = 4 * D
    R = 2 * NY
    C = 2 * NT
    M = NT * R
    dp = lax.axis_index("dp")
    t = lax.axis_index("tensor")
    c = lax.rem(dp, 2)
    y = lax.rem(lax.div(dp, 2), NY)
    z = lax.div(dp, 2 * NY)

    def at(zz, yy, cc):
        return ((zz * NY + yy) * 2 + cc, t)

    core = at(z, y, 1 - c)
    zed = at(1 - z, y, c)

    def up_y(r):
        return lax.rem(y + r + NY, NY)

    def up_t(r):
        return lax.rem(t + r, NT)

    ypeers = [at(z, up_y(r), c) for r in range(1, NY)]
    tpeers = [(dp, up_t(r)) for r in range(1, NT)]
    left, right = at(z, up_y(-1), c), at(z, up_y(1), c)

    barrier = pltpu.get_barrier_semaphore()
    peers = [core, zed] + ypeers + tpeers
    for peer in peers:
        pl.semaphore_signal(barrier, inc=1, device_id=peer, device_id_type=MESH)

    links = []
    count = [0]

    def send(src, dst, device):
        link = Link((send_sems, recv_sems), count[0], src, dst, device)
        count[0] += 1
        links.append(link)
        return link

    def rows(q):
        return pl.ds(pl.multiple_of(q * D, 16), D)

    def chunk(j, size):
        return pl.ds(pl.multiple_of(j * size, size), size)

    row = lax.broadcasted_iota(jnp.int32, (R, KP), 0)
    lane = lax.broadcasted_iota(jnp.int32, (R, KP), 1)
    for j in range(NY):
        a = xs[j]
        a = jnp.where(row == 2 * y, a[0:1], jnp.where(row == 2 * y + 1, a[1:2], 0.0))
        hi = a.astype(BF).astype(F32)
        mid = (a - hi).astype(BF).astype(F32)
        low = a - hi - mid
        stage[j] = jnp.where(lane == K + 1, mid, jnp.where(lane == K + 2, low, hi)).astype(BF)
    pl.semaphore_wait(barrier, len(peers))

    xa = [send(stage.at[up_y(r)], xin.at[r - 1], ypeers[r - 1]) for r in range(1, NY)]

    own, other = z * 2 + c, (1 - z) * 2 + c
    mats = (wg, wu, vg, vu, wd, vd)
    locals_, from_core, from_z = [], [], []
    for k, m in enumerate(mats):
        dst = W.at[k, rows(own)]
        cp = pltpu.make_async_copy(m, dst, local_sems.at[k])
        cp.start()
        locals_.append(cp)
        from_z.append(send(m, dst, zed))
        from_core.append(send(m, dst, core))
    if KP > K:
        for k in range(6):
            W[k, K:KP, :] = jnp.zeros((KP - K, F), BF)

    x16 = stage[y].astype(F32)
    for r in range(1, NY):
        xa[r - 1].arrive()
        x16 = x16 + xin[r - 1].astype(F32)
    curv = x16[:, K : K + 1] + x16[:, K + 1 : K + 2] + x16[:, K + 2 : K + 3]
    X[chunk(t, R)] = x16.astype(BF)
    xg = [send(X.at[chunk(t, R)], X.at[chunk(t, R)], p) for p in tpeers]

    forwards = {}

    def forward(k):
        from_z[k].arrive()
        forwards[k] = send(W.at[k, rows(other)], W.at[k, rows(other)], core)

    def have(k):
        locals_[k].wait()
        from_core[k].arrive()
        forwards[k].arrive()

    forward(0)
    for link in xg:
        link.arrive()
    x = X[...]

    def reduce_scatter(n, begin, part, own_part, sendbuf, recvbuf, hops, between=None):
        got = {}
        waves = {}
        for k in range(n):
            for s in range(1, max(hops[k]) + 1):
                waves.setdefault(k + s if begin else s, []).append((k, s))
        for w in sorted(waves):
            for k, s in sorted(waves[w]):
                if s == 1 and begin:
                    begin(k)
                for side in (0, 1):
                    n_hops = hops[k][side]
                    if s > n_hops:
                        continue
                    far = n_hops - s + 1
                    j = up_y(-far) if side == 0 else up_y(far)
                    v = part(k, j)
                    if s > 1:
                        got[k, side, s - 1].arrive()
                        v = v + recvbuf[k, side, s - 2].astype(F32)
                    sendbuf[k, side, s - 1] = v.astype(BF)
                    got[k, side, s] = send(
                        sendbuf.at[k, side, s - 1], recvbuf.at[k, side, s - 1], left if side == 0 else right
                    )
            if between and w in between:
                between[w]()
        out = []
        for k in range(n):
            v = own_part(k)
            for side in (0, 1):
                if hops[k][side]:
                    got[k, side, hops[k][side]].arrive()
                    v = v + recvbuf[k, side, hops[k][side] - 1].astype(F32)
            out.append(v)
        return out

    def all_gather(n, buf, hops):
        got = {}
        for s in range(1, max(max(h) for h in hops) + 1):
            for k in range(n):
                for side in (0, 1):
                    if s > hops[k][side]:
                        continue
                    if s > 1:
                        got[k, side, s - 1].arrive()
                    origin = up_y(s - 1) if side == 0 else up_y(1 - s)
                    ref = buf.at[k, chunk(origin, C)]
                    got[k, side, s] = send(ref, ref, left if side == 0 else right)

        def finish(k):
            for side in (0, 1):
                if hops[k][side]:
                    got[k, side, hops[k][side]].arrive()

        return finish

    long, short = NY // 2, NY // 2 - 1
    both = [(long, short), (short, long)] * 2

    def begin(k):
        have(k)
        Pf[k] = dot(x, W[k], 1, 0)
        if k + 1 < 4:
            forward(k + 1)

    gate, up, dgate, dup = reduce_scatter(
        4, begin, lambda k, j: Pf[k, chunk(j, C)], lambda k: Pf[k, chunk(y, C)], rs_s, rs_r, both
    )
    sig = jax.nn.sigmoid(gate)
    act = gate * sig
    slope = sig * (1.0 + gate * (1.0 - sig))
    H[0, chunk(y, C)] = (act * up).astype(BF)
    H[1, chunk(y, C)] = (slope * dgate * up + act * dup).astype(BF)
    finish = all_gather(2, H, both)
    forward(4)
    forward(5)
    have(4)
    have(5)
    finish(0)
    tangent = dot(H[0], W[5], 1, 1)
    finish(1)
    tangent = tangent + dot(H[1], W[4], 1, 1)

    Tf[...] = tangent
    Tb[...] = tangent.astype(BF)
    tr = [send(Tb.at[chunk(up_t(r), R)], trecv.at[r - 1], tpeers[r - 1]) for r in range(1, NT)]
    total = Tf[chunk(t, R)]
    for r in range(1, NT):
        tr[r - 1].arrive()
        total = total + trecv[r - 1].astype(F32)
    wt[chunk(t, R)] = (curv * total).astype(BF)
    tw = [send(wt.at[chunk(t, R)], wt.at[chunk(t, R)], p) for p in tpeers]
    osend[...] = total.astype(BF)
    oa = [send(osend, orecv.at[r - 1], ypeers[r - 1]) for r in range(1, NY)]
    for link in tw:
        link.arrive()
    weighted = wt[...]

    Pd[...] = dot(weighted, W[4], 1, 0)
    half = C // 2

    def part_of(k, j):
        return Pd[pl.ds(pl.multiple_of(j * C + k * half, half), half)]

    stage1, stage2 = {}, {}

    def product(i, lhs, rhs):
        full = dot(lhs, rhs, 0, 0)
        PF[i] = full
        PB[i] = full.astype(BF)
        for n, zz in enumerate((1 - z, z)):
            stage1[i, n] = send(PB.at[i, rows(zz * 2 + 1 - c)], C1.at[i, n], core)

    def cross(i):
        stage1[i, 0].arrive()
        zs[i] = (PF[i, rows((1 - z) * 2 + c)] + C1[i, 0].astype(F32)).astype(BF)
        stage2[i] = send(zs.at[i], zr.at[i], zed)

    def settle(i, out):
        stage1[i, 1].arrive()
        mine = PF[i, rows(z * 2 + c)] + C1[i, 1].astype(F32)
        stage2[i].arrive()
        out[...] = mine + zr[i].astype(F32)

    def early():
        product(2, weighted, H[0])

    halves = reduce_scatter(
        2, None, part_of, lambda k: part_of(k, y), dh_s, dh_r, both, {1: early}
    )
    dhid = jnp.concatenate(halves, axis=0)
    B[0, chunk(y, C)] = (dhid * up * slope).astype(BF)
    B[1, chunk(y, C)] = (dhid * act).astype(BF)
    finish = all_gather(2, B, both)
    cross(2)

    def two_rows(v):
        v = v.astype(F32)
        return [jnp.sum(jnp.where(row == 2 * y + i, v, 0.0), axis=0, keepdims=True) for i in (0, 1)]

    for r in range(NY):
        if r:
            oa[r - 1].arrive()
        a, b = two_rows(orecv[r - 1] if r else osend[...])
        j = up_y(-r)
        to[j, 0:1, :] = a
        to[j, 1:2, :] = b
    settle(2, pd)

    finish(0)
    product(0, x, B[0])
    finish(1)
    product(1, x, B[1])
    cross(0)
    cross(1)
    settle(0, pg)
    settle(1, pu)
    for link in links:
        link.left()


def on_device(NY, NT, inputs, curvature, w_gate, w_up, w_down, v_gate, v_up, v_down):
    D, F = w_gate.shape
    K = 4 * D
    KP = -(-(K + 3) // 128) * 128
    R, C = 2 * NY, 2 * NT
    M = NT * R
    long = NY // 2
    xs = inputs.reshape(2, 2, NY, 2 * D).transpose(2, 0, 1, 3).reshape(NY, 2, K).astype(F32)
    xs = jnp.concatenate([xs, jnp.broadcast_to(curvature[None, :, None], (NY, 2, KP - K))], axis=2)
    n_links = 2 * (NY - 1) + 3 * (NT - 1) + 18 + 9 + 10 * (NY - 1)
    vmem = pl.BlockSpec(memory_space=pltpu.VMEM)
    hbm = pl.BlockSpec(memory_space=pl.ANY)
    to, pg, pu, pd = pl.pallas_call(
        functools.partial(kernel, NY, NT, D, F, KP),
        out_shape=[
            jax.ShapeDtypeStruct((NY, 2, KP), F32),
            jax.ShapeDtypeStruct((D, F), F32),
            jax.ShapeDtypeStruct((D, F), F32),
            jax.ShapeDtypeStruct((D, F), F32),
        ],
        in_specs=[vmem] + [hbm] * 6,
        out_specs=[vmem] * 4,
        scratch_shapes=[
            pltpu.VMEM((NY, R, KP), BF),
            pltpu.VMEM((NY - 1, R, KP), BF),
            pltpu.VMEM((M, KP), BF),
            pltpu.VMEM((6, KP, F), BF),
            pltpu.VMEM((4, M, F), F32),
            pltpu.VMEM((M, F), F32),
            pltpu.VMEM((4, 2, long, C, F), BF),
            pltpu.VMEM((4, 2, long, C, F), BF),
            pltpu.VMEM((2, 2, long, C // 2, F), BF),
            pltpu.VMEM((2, 2, long, C // 2, F), BF),
            pltpu.VMEM((2, M, F), BF),
            pltpu.VMEM((2, M, F), BF),
            pltpu.VMEM((M, KP), F32),
            pltpu.VMEM((M, KP), BF),
            pltpu.VMEM((max(NT - 1, 1), R, KP), BF),
            pltpu.VMEM((M, KP), BF),
            pltpu.VMEM((R, KP), BF),
            pltpu.VMEM((NY - 1, R, KP), BF),
            pltpu.VMEM((3, KP, F), F32),
            pltpu.VMEM((3, KP, F), BF),
            pltpu.VMEM((3, 2, D, F), BF),
            pltpu.VMEM((3, D, F), BF),
            pltpu.VMEM((3, D, F), BF),
            pltpu.SemaphoreType.DMA((n_links,)),
            pltpu.SemaphoreType.DMA((n_links,)),
            pltpu.SemaphoreType.DMA((6,)),
        ],
        compiler_params=pltpu.CompilerParams(
            collective_id=0, has_side_effects=True, vmem_limit_bytes=48 * 1024 * 1024
        ),
    )(xs, w_gate, w_up, v_gate, v_up, w_down.T, v_down.T)
    out = to[:, :, :K].reshape(NY, 2, 2, 2 * D).transpose(1, 2, 0, 3).reshape(2, 4 * NY * D)
    return out.astype(BF), pg, pu, pd.T


def solution(mesh):
    ndp, nt = mesh.shape["dp"], mesh.shape["tensor"]
    return jax.shard_map(
        functools.partial(on_device, ndp // 4, nt),
        mesh=mesh,
        in_specs=(
            P(("dp", "tensor"), None),
            P(("dp", "tensor")),
            P("dp", "tensor"),
            P("dp", "tensor"),
            P("tensor", "dp"),
            P("dp", "tensor"),
            P("dp", "tensor"),
            P("tensor", "dp"),
        ),
        out_specs=(
            P(("dp", "tensor"), None),
            P("dp", "tensor"),
            P("dp", "tensor"),
            P("tensor", "dp"),
        ),
        check_vma=False,
    )
```

time: 827 us -> 155 us (0.19)
  waiting for transfers between devices: 666 us -> 0 us
  Pallas kernels: 0 us -> 145 us
  blocking collectives: 81 us -> 0 us
  matrix products: 31.5 us -> 0 us
  starting transfers between devices: 27.4 us -> 0 us
  between operations: 14.9 us -> 0.67 us
    all_gather x9 -> x0, waiting for transfers between devices: 493 us -> none  [the longest x2 134 us: on_device(): pieces = lax.all_gather((w_down, v_down), 'dp', axis=1, tiled=True)]
    unnamed x11 -> x0, waiting for transfers between devices: 153 us -> none
    pallas_call x0 -> x1, Pallas kernels: none -> 145 us  [on_device(): pl.pallas_call(functools.partial(kernel, NY, NT, D, F, KP), out_shape=[ja...]
    all_gather x2 -> x0, blocking collectives: 81 us -> none  [the longest x1 44.6 us: on_device(): lax.all_gather(inputs, 'tensor', axis=0, tiled=True)]
    dot_general x9 -> x0, matrix products: 31.5 us -> none  [the longest x3 9.45 us: on_device(): jnp.dot(cols, p, preferred_element_type=jnp.float32)]
    all_to_all x2 -> x0, starting transfers between devices: 27.1 us -> none  [the longest x1 21.8 us: on_device(): lax.all_to_all(weighted_all, 'dp', split_axis=1, concat_axis=0, tiled=True)]
    all_to_all x2 -> x0, waiting for transfers between devices: 20.4 us -> none  [the longest x1 11.1 us: on_device(): lax.all_to_all(weighted_all, 'dp', split_axis=1, concat_axis=0, tiled=True)]
  transfers between devices with their start and end apart: 12 -> 0, of which waited for: 11 -> 0; matrix products, arithmetic and copies ran while one was open for 3% -> 0% of each run, Pallas kernels for 0% -> 0%
where the time goes in v1:
time: 155 us
  Pallas kernels  145 us (94%)
  local copies, waits for them, and re-layouts  9.15 us (6%)
    pallas_call x1, Pallas kernels, on_device(): pl.pallas_call(functools.partial(kernel, NY, NT, D, F, KP), out_shape=[ja...  145 us
    unnamed x15, local copies, waits for them, and re-layouts  6.67 us

profile of v1, /device:TPU:1, one launch (start us, length us, event | category | flops | bytes accessed | tf_op | source)
XLA Modules:
  0.0 154.8 jit_solution(7594512921896466882)
XLA Ops:
  0.6 0.0 copy-start
  0.6 0.8 broadcast_in_dim.2
  1.4 0.8 reshape.20
  2.2 0.1 reshape.19
  2.3 0.1 pad_maximum_fusion.xs
  2.4 0.0 copy-done
  2.4 0.0 copy-start.1
  2.4 0.9 copy-done.1
  3.3 0.0 copy-start.2
  3.3 0.9 copy-done.2
  4.2 0.0 copy-start.3
  4.2 0.9 copy-done.3
  5.1 0.0 copy-start.4
  5.1 0.9 copy-done.4
  6.0 0.0 copy-start.5
  6.0 0.9 copy-done.5
  6.9 144.9 %shard_map.111 = (f32[8,2,384]{2,1,0:T(2,128)S(1)}, f32[80,864]{1,0:T(8,128)S(1)}, f32[80,864]{1,0:T(8,128)S(1)}, f32[80,864]{1,0:T(8,128)S(1)}) custom-call(f32[8,2,384]{2,1,0:T(2,128)S(1)} %pad_maximum_fusion.xs, bf16[80,864]{1,0:T(8,128)(2,1)S(1)} %copy-done, bf16[80,864]{1,0:T(8,128)(2,1)S(1)} %copy-done.1, bf16[80,864]{1,0:T(8,128)(2,1)S(1)} %copy-done.2, ...), custom_call_target="tpu_custom_call" | custom-call | tf_op jit(solution)/shard_map/pallas_call | solution.py:316
  151.9 0.1 convert_element_type.26
  152.0 0.7 convert_element_type.28
  152.7 0.7 copy.19
  153.4 0.7 copy.20
  154.1 0.7 copy.21
  (3 shorter events, 0.0 us)
Async XLA Ops:
  0.6 1.8 %copy-start = (bf16[80,864]{1,0:T(8,128)(2,1)S(1)}, bf16[80,864]{1,0:T(8,128)(2,1)}, u32[]{:S(2)}) copy-start(bf16[80,864]{1,0:T(8,128)(2,1)} %wg.1) | copy-start | bytes 414724
  2.4 0.9 copy-start.1
  3.3 0.9 copy-start.2
  4.2 0.9 copy-start.3
  5.1 0.9 copy-start.4
  6.0 0.9 copy-start.5

commit v2 on v1

--- a/solution.py
+++ b/solution.py
@@ -37,16 +37,18 @@
 
 def kernel(
     NY, NT, D, F, KP,
-    xs, wg, wu, vg, vu, wd, vd,
+    x_in, curv_in, wg, wu, vg, vu, wd, vd,
     to, pg, pu, pd,
     stage, xin, X, W, Pf, Pd, rs_s, rs_r, dh_s, dh_r, H, B,
-    Tf, Tb, trecv, wt, osend, orecv, PF, PB, C1, zs, zr,
+    Tf, Tb, trecv, wt, osend, orecv, ot, PF, PB, C1, zs, zr,
     send_sems, recv_sems, local_sems,
 ):
     K = 4 * D
     R = 2 * NY
     C = 2 * NT
     M = NT * R
+    NX = 4 if NT % 4 == 0 else 1
+    NH = NT // NX
     dp = lax.axis_index("dp")
     t = lax.axis_index("tensor")
     c = lax.rem(dp, 2)
@@ -67,6 +69,13 @@
 
     ypeers = [at(z, up_y(r), c) for r in range(1, NY)]
     tpeers = [(dp, up_t(r)) for r in range(1, NT)]
+    xq, h = lax.rem(t, NX), lax.div(t, NX)
+
+    def up_h(r):
+        return lax.rem(h + r, NH) * NX + xq
+
+    hpeers = [(dp, up_h(r)) for r in range(1, NH)]
+    xpeers = [(dp, h * NX + lax.rem(xq + r, NX)) for r in range(1, NX)]
     left, right = at(z, up_y(-1), c), at(z, up_y(1), c)
 
     barrier = pltpu.get_barrier_semaphore()
@@ -91,8 +100,12 @@
 
     row = lax.broadcasted_iota(jnp.int32, (R, KP), 0)
     lane = lax.broadcasted_iota(jnp.int32, (R, KP), 1)
+    raw = x_in[...].astype(F32)
+    tail = lax.broadcasted_iota(jnp.int32, (2, KP - K), 0)
+    tail = jnp.where(tail == 0, curv_in[0], curv_in[1])
     for j in range(NY):
-        a = xs[j]
+        parts = [raw[:, (zz * NY + j) * 2 * D : (zz * NY + j + 1) * 2 * D] for zz in (0, 1)]
+        a = jnp.concatenate(parts + [tail], axis=1)
         a = jnp.where(row == 2 * y, a[0:1], jnp.where(row == 2 * y + 1, a[1:2], 0.0))
         hi = a.astype(BF).astype(F32)
         mid = (a - hi).astype(BF).astype(F32)
@@ -104,14 +117,26 @@
 
     own, other = z * 2 + c, (1 - z) * 2 + c
     mats = (wg, wu, vg, vu, wd, vd)
-    locals_, from_core, from_z = [], [], []
-    for k, m in enumerate(mats):
+    locals_, from_core, from_z, forwards = {}, {}, {}, {}
+
+    def fetch(k):
         dst = W.at[k, rows(own)]
-        cp = pltpu.make_async_copy(m, dst, local_sems.at[k])
-        cp.start()
-        locals_.append(cp)
-        from_z.append(send(m, dst, zed))
-        from_core.append(send(m, dst, core))
+        from_z[k] = send(mats[k], dst, zed)
+        from_core[k] = send(mats[k], dst, core)
+        locals_[k] = pltpu.make_async_copy(mats[k], dst, local_sems.at[k])
+        locals_[k].start()
+
+    def forward(k):
+        from_z[k].arrive()
+        forwards[k] = send(W.at[k, rows(other)], W.at[k, rows(other)], core)
+
+    def have(k):
+        locals_[k].wait()
+        from_core[k].arrive()
+        forwards[k].arrive()
+
+    fetch(0)
+    fetch(1)
     if KP > K:
         for k in range(6):
             W[k, K:KP, :] = jnp.zeros((KP - K, F), BF)
@@ -122,30 +147,38 @@
         x16 = x16 + xin[r - 1].astype(F32)
     curv = x16[:, K : K + 1] + x16[:, K + 1 : K + 2] + x16[:, K + 2 : K + 3]
     X[chunk(t, R)] = x16.astype(BF)
-    xg = [send(X.at[chunk(t, R)], X.at[chunk(t, R)], p) for p in tpeers]
-
-    forwards = {}
-
-    def forward(k):
-        from_z[k].arrive()
-        forwards[k] = send(W.at[k, rows(other)], W.at[k, rows(other)], core)
-
-    def have(k):
-        locals_[k].wait()
-        from_core[k].arrive()
-        forwards[k].arrive()
-
+
+    def all_tensor(buf):
+        got = [send(buf.at[chunk(t, R)], buf.at[chunk(t, R)], p) for p in hpeers]
+
+        def second():
+            block = {}
+            mine = [buf.at[chunk(t, R)]] + [buf.at[chunk(up_h(r), R)] for r in range(1, NH)]
+            for n, ref in enumerate(mine):
+                if n:
+                    got[NH - 1 - n].arrive()
+                for p in xpeers:
+                    block[n, len(block)] = send(ref, ref, p)
+            return list(block.values())
+
+        return second
+
+    second = all_tensor(X)
+    fetch(2)
+    xg = second()
+    fetch(3)
     forward(0)
+    forward(1)
     for link in xg:
         link.arrive()
     x = X[...]
 
-    def reduce_scatter(n, begin, part, own_part, sendbuf, recvbuf, hops, between=None):
+    def reduce_scatter(n, begin, part, own_part, sendbuf, recvbuf, hops, skew, between=None):
         got = {}
         waves = {}
         for k in range(n):
             for s in range(1, max(hops[k]) + 1):
-                waves.setdefault(k + s if begin else s, []).append((k, s))
+                waves.setdefault(skew[k] + s, []).append((k, s))
         for w in sorted(waves):
             for k, s in sorted(waves[w]):
                 if s == 1 and begin:
@@ -202,11 +235,12 @@
     def begin(k):
         have(k)
         Pf[k] = dot(x, W[k], 1, 0)
-        if k + 1 < 4:
+        if k in (1, 2):
             forward(k + 1)
 
     gate, up, dgate, dup = reduce_scatter(
-        4, begin, lambda k, j: Pf[k, chunk(j, C)], lambda k: Pf[k, chunk(y, C)], rs_s, rs_r, both
+        4, begin, lambda k, j: Pf[k, chunk(j, C)], lambda k: Pf[k, chunk(y, C)], rs_s, rs_r, both, (0, 0, 1, 2),
+        {3: lambda: fetch(4), 4: lambda: fetch(5)},
     )
     sig = jax.nn.sigmoid(gate)
     act = gate * sig
@@ -268,7 +302,7 @@
         product(2, weighted, H[0])
 
     halves = reduce_scatter(
-        2, None, part_of, lambda k: part_of(k, y), dh_s, dh_r, both, {1: early}
+        2, None, part_of, lambda k: part_of(k, y), dh_s, dh_r, both, (0, 0), {1: early}
     )
     dhid = jnp.concatenate(halves, axis=0)
     B[0, chunk(y, C)] = (dhid * up * slope).astype(BF)
@@ -284,9 +318,11 @@
         if r:
             oa[r - 1].arrive()
         a, b = two_rows(orecv[r - 1] if r else osend[...])
-        j = up_y(-r)
-        to[j, 0:1, :] = a
-        to[j, 1:2, :] = b
+        ot[up_y(-r)] = jnp.concatenate([a, b], axis=0)
+    for j in range(NY):
+        v = ot[j].astype(BF)
+        for zz in (0, 1):
+            to[:, (zz * NY + j) * 2 * D : (zz * NY + j + 1) * 2 * D] = v[:, zz * 2 * D : (zz + 1) * 2 * D]
     settle(2, pd)
 
     finish(0)
@@ -308,20 +344,18 @@
     R, C = 2 * NY, 2 * NT
     M = NT * R
     long = NY // 2
-    xs = inputs.reshape(2, 2, NY, 2 * D).transpose(2, 0, 1, 3).reshape(NY, 2, K).astype(F32)
-    xs = jnp.concatenate([xs, jnp.broadcast_to(curvature[None, :, None], (NY, 2, KP - K))], axis=2)
     n_links = 2 * (NY - 1) + 3 * (NT - 1) + 18 + 9 + 10 * (NY - 1)
     vmem = pl.BlockSpec(memory_space=pltpu.VMEM)
     hbm = pl.BlockSpec(memory_space=pl.ANY)
     to, pg, pu, pd = pl.pallas_call(
         functools.partial(kernel, NY, NT, D, F, KP),
         out_shape=[
-            jax.ShapeDtypeStruct((NY, 2, KP), F32),
+            jax.ShapeDtypeStruct((2, 4 * NY * D), BF),
             jax.ShapeDtypeStruct((D, F), F32),
             jax.ShapeDtypeStruct((D, F), F32),
             jax.ShapeDtypeStruct((D, F), F32),
         ],
-        in_specs=[vmem] + [hbm] * 6,
+        in_specs=[vmem, pl.BlockSpec(memory_space=pltpu.SMEM)] + [hbm] * 6,
         out_specs=[vmem] * 4,
         scratch_shapes=[
             pltpu.VMEM((NY, R, KP), BF),
@@ -342,6 +376,7 @@
             pltpu.VMEM((M, KP), BF),
             pltpu.VMEM((R, KP), BF),
             pltpu.VMEM((NY - 1, R, KP), BF),
+            pltpu.VMEM((NY, 2, KP), F32),
             pltpu.VMEM((3, KP, F), F32),
             pltpu.VMEM((3, KP, F), BF),
             pltpu.VMEM((3, 2, D, F), BF),
@@ -352,11 +387,10 @@
             pltpu.SemaphoreType.DMA((6,)),
         ],
         compiler_params=pltpu.CompilerParams(
-            collective_id=0, has_side_effects=True, vmem_limit_bytes=48 * 1024 * 1024
+            collective_id=0, has_side_effects=True, vmem_limit_bytes=62 * 1024 * 1024
         ),
-    )(xs, w_gate, w_up, v_gate, v_up, w_down.T, v_down.T)
-    out = to[:, :, :K].reshape(NY, 2, 2, 2 * D).transpose(1, 2, 0, 3).reshape(2, 4 * NY * D)
-    return out.astype(BF), pg, pu, pd.T
+    )(inputs, curvature, w_gate, w_up, v_gate, v_up, w_down.T, v_down.T)
+    return to, pg, pu, pd.T
 
 
 def solution(mesh):

time: 155 us -> 137 us (0.88)
  Pallas kernels: 145 us -> 131 us
  local copies, waits for them, and re-layouts: 9.15 us -> 4.82 us
    pallas_call x1, Pallas kernels: 145 us -> 131 us  [on_device(): pl.pallas_call(functools.partial(kernel, NY, NT, D, F, KP), out_shape=[ja...]
    unnamed x15 -> x8, local copies, waits for them, and re-layouts: 6.67 us -> 4.82 us
    convert_element_type x6 -> x0, local copies, waits for them, and re-layouts: 1.7 us -> none  [the longest x3 0.91 us: on_device(): inputs.reshape(2, 2, NY, 2 * D).transpose(2, 0, 1, 3).reshape(NY, 2, K)]
where the time goes in v2:
time: 137 us
  Pallas kernels  131 us (96%)
  local copies, waits for them, and re-layouts  4.82 us (4%)
    pallas_call x1, Pallas kernels, on_device(): pl.pallas_call(functools.partial(kernel, NY, NT, D, F, KP), out_shape=[ja...  131 us
    unnamed x8, local copies, waits for them, and re-layouts  4.82 us

profile of v2, /device:TPU:1, one launch (start us, length us, event | category | flops | bytes accessed | tf_op | source)
XLA Modules:
  0.0 136.8 jit_solution(1426993491371390507)
XLA Ops:
  0.6 131.3 %shard_map.111 = (bf16[2,2560]{1,0:T(2,128)(2,1)}, f32[80,864]{1,0:T(8,128)}, f32[80,864]{1,0:T(8,128)}, f32[80,864]{1,0:T(8,128)}) custom-call(bf16[2,2560]{1,0:T(2,128)(2,1)} %x_in.1, f32[2]{0:T(128)} %curv_in.1, bf16[80,864]{1,0:T(8,128)(2,1)} %wg.1, bf16[80,864]{1,0:T(8,128)(2,1)} %wu.1, bf16[80,864]{1,0:T(8,128)(2,1)} %vg.1, bf16[80,864]{1,0:T(8,128)(2,1)} %vu.1, ...), custom_call_target="tpu_custom_call" | custom-call | tf_op jit(solution)/shard_map/pallas_call | solution.py:350
  132.0 1.3 copy.16
  133.3 0.0 copy-start.1
  133.3 1.7 %copy.17 = f32[80,864]{1,0:T(8,128)} copy(f32[80,864]{1,0:T(8,128)} %get-tuple-element.17) | data formatting | bytes 552960
  135.0 0.0 copy-done.1
  135.0 0.0 copy-start
  135.0 0.7 copy.18
  135.7 0.3 copy-done
  136.1 0.7 copy.19
Async XLA Ops:
  133.3 1.7 %copy-start.1 = (f32[80,864]{1,0:T(8,128)S(1)}, f32[80,864]{1,0:T(8,128)}, u32[]{:S(2)}) copy-start(f32[80,864]{1,0:T(8,128)} %get-tuple-element.18) | copy-start | bytes 829444
  135.0 1.1 copy-start

commit v3 on v2

--- a/solution.py
+++ b/solution.py
@@ -39,7 +39,7 @@
     NY, NT, D, F, KP,
     x_in, curv_in, wg, wu, vg, vu, wd, vd,
     to, pg, pu, pd,
-    stage, xin, X, W, Pf, Pd, rs_s, rs_r, dh_s, dh_r, H, B,
+    stage, xin, X, W, Pf, Pd, rs_s, rs_r, dh_s, dh_r, H, A, G,
     Tf, Tb, trecv, wt, osend, orecv, ot, PF, PB, C1, zs, zr,
     send_sems, recv_sems, local_sems,
 ):
@@ -76,7 +76,6 @@
 
     hpeers = [(dp, up_h(r)) for r in range(1, NH)]
     xpeers = [(dp, h * NX + lax.rem(xq + r, NX)) for r in range(1, NX)]
-    left, right = at(z, up_y(-1), c), at(z, up_y(1), c)
 
     barrier = pltpu.get_barrier_semaphore()
     peers = [core, zed] + ypeers + tpeers
@@ -173,64 +172,127 @@
         link.arrive()
     x = X[...]
 
-    def reduce_scatter(n, begin, part, own_part, sendbuf, recvbuf, hops, skew, between=None):
+    def dist(d, n):
+        return at(z, up_y(d * n), c)
+
+    def reach(k, d):
+        return NY // 2 - (1 if (k % 2 == 0) == (d > 0) else 0)
+
+    def reduce_ring(k, part, sent, recv):
         got = {}
-        waves = {}
-        for k in range(n):
-            for s in range(1, max(hops[k]) + 1):
-                waves.setdefault(skew[k] + s, []).append((k, s))
-        for w in sorted(waves):
-            for k, s in sorted(waves[w]):
-                if s == 1 and begin:
-                    begin(k)
-                for side in (0, 1):
-                    n_hops = hops[k][side]
-                    if s > n_hops:
-                        continue
-                    far = n_hops - s + 1
-                    j = up_y(-far) if side == 0 else up_y(far)
-                    v = part(k, j)
-                    if s > 1:
-                        got[k, side, s - 1].arrive()
-                        v = v + recvbuf[k, side, s - 2].astype(F32)
-                    sendbuf[k, side, s - 1] = v.astype(BF)
-                    got[k, side, s] = send(
-                        sendbuf.at[k, side, s - 1], recvbuf.at[k, side, s - 1], left if side == 0 else right
-                    )
-            if between and w in between:
-                between[w]()
-        out = []
-        for k in range(n):
-            v = own_part(k)
-            for side in (0, 1):
-                if hops[k][side]:
-                    got[k, side, hops[k][side]].arrive()
-                    v = v + recvbuf[k, side, hops[k][side] - 1].astype(F32)
-            out.append(v)
-        return out
-
-    def all_gather(n, buf, hops):
+
+        def step(s):
+            for i, d in enumerate((-1, 1)):
+                n = reach(k, d)
+                if s > n:
+                    continue
+                v = part(k, up_y(d * (n - s + 1)))
+                if s > 1:
+                    got[i].arrive()
+                    v = v + recv[k, i, s - 2].astype(F32)
+                sent[k, i, s - 1] = v.astype(BF)
+                got[i] = send(sent.at[k, i, s - 1], recv.at[k, i, s - 1], dist(d, 1))
+
+        def total():
+            v = part(k, y)
+            for i, d in enumerate((-1, 1)):
+                if reach(k, d):
+                    got[i].arrive()
+                    v = v + recv[k, i, reach(k, d) - 1].astype(F32)
+            return v
+
+        return {s: functools.partial(step, s) for s in range(1, NY // 2 + 1)}, total
+
+    def reduce_tree(k, part, sent, recv):
         got = {}
-        for s in range(1, max(max(h) for h in hops) + 1):
-            for k in range(n):
-                for side in (0, 1):
-                    if s > hops[k][side]:
-                        continue
-                    if s > 1:
-                        got[k, side, s - 1].arrive()
-                    origin = up_y(s - 1) if side == 0 else up_y(1 - s)
-                    ref = buf.at[k, chunk(origin, C)]
-                    got[k, side, s] = send(ref, ref, left if side == 0 else right)
-
-        def finish(k):
-            for side in (0, 1):
-                if hops[k][side]:
-                    got[k, side, hops[k][side]].arrive()
-
-        return finish
-
-    long, short = NY // 2, NY // 2 - 1
-    both = [(long, short), (short, long)] * 2
+
+        def push(i, d, slot, v, far):
+            sent[k, i, slot] = v.astype(BF)
+            got[i, slot] = send(sent.at[k, i, slot], recv.at[k, i, slot], dist(d, far))
+
+        def first():
+            for i, d in enumerate((-1, 1)):
+                if reach(k, d) == 4:
+                    push(i, d, 0, part(k, up_y(4 * d)), 2)
+                push(i, d, 1, part(k, up_y(3 * d)), 1)
+            for i, d in enumerate((-1, 1)):
+                push(i, d, 2, part(k, up_y(d)), 1)
+
+        def second():
+            for i, d in enumerate((-1, 1)):
+                v = part(k, up_y(2 * d))
+                for slot in (1, 0) if reach(k, d) == 4 else (1,):
+                    got[i, slot].arrive()
+                    v = v + recv[k, i, slot].astype(F32)
+                push(i, d, 3, v, 2)
+
+        def total():
+            v = part(k, y)
+            for slot in (2, 3):
+                for i in (0, 1):
+                    got[i, slot].arrive()
+                    v = v + recv[k, i, slot].astype(F32)
+            return v
+
+        return {1: first, 2: second}, total
+
+    def gather_ring(k, ref):
+        got = {}
+
+        def step(s):
+            for i, d in enumerate((-1, 1)):
+                if s > reach(k, d):
+                    continue
+                if s > 1:
+                    got[i].arrive()
+                block = ref(up_y(-d * (s - 1)))
+                got[i] = send(block, block, dist(d, 1))
+
+        def finish():
+            for i in got:
+                got[i].arrive()
+
+        return {s: functools.partial(step, s) for s in range(1, NY // 2 + 1)}, finish
+
+    def gather_tree(k, ref):
+        got = {}
+
+        def first():
+            for far in (2, 1):
+                for i, d in enumerate((-1, 1)):
+                    got[i, 2 - far] = send(ref(y), ref(y), dist(d, far))
+
+        def second():
+            for i, d in enumerate((-1, 1)):
+                got[i, 0].arrive()
+                block = ref(up_y(-2 * d))
+                if reach(k, d) == 4:
+                    got[i, 3] = send(block, block, dist(d, 2))
+                got[i, 2] = send(block, block, dist(d, 1))
+
+        def finish():
+            for i, slot in got:
+                if slot:
+                    got[i, slot].arrive()
+
+        return {1: first, 2: second}, finish
+
+    def in_waves(plans, late=None, between=None):
+        steps = []
+        for n, (waves, _) in enumerate(plans):
+            steps += [(w + (late[n] if late else 0), n, f) for w, f in waves.items()]
+        last = None
+        for w, n, f in sorted(steps, key=lambda e: e[:2]):
+            if between and last is not None and w != last and last in between:
+                between[last]()
+            last = w
+            f()
+
+    if NY != 8:
+        reduce_tree, gather_tree = reduce_ring, gather_ring
+
+    def part(k, j):
+        return Pf[k, chunk(j, C)]
 
     def begin(k):
         have(k)
@@ -238,28 +300,55 @@
         if k in (1, 2):
             forward(k + 1)
 
-    gate, up, dgate, dup = reduce_scatter(
-        4, begin, lambda k, j: Pf[k, chunk(j, C)], lambda k: Pf[k, chunk(y, C)], rs_s, rs_r, both, (0, 0, 1, 2),
-        {3: lambda: fetch(4), 4: lambda: fetch(5)},
-    )
+    plans = []
+    for k in range(4):
+        waves, total = reduce_ring(k, part, rs_s, rs_r)
+
+        def opened(k=k, step=waves[1]):
+            begin(k)
+            step()
+
+        waves[1] = opened
+        plans.append((waves, total))
+
+    def down():
+        fetch(4)
+        fetch(5)
+
+    in_waves(plans, (0, 0, 1, 2), {2: down})
+    gate, up, dgate, dup = [total() for _, total in plans]
     sig = jax.nn.sigmoid(gate)
     act = gate * sig
     slope = sig * (1.0 + gate * (1.0 - sig))
+    up_slope = up * slope
     H[0, chunk(y, C)] = (act * up).astype(BF)
-    H[1, chunk(y, C)] = (slope * dgate * up + act * dup).astype(BF)
-    finish = all_gather(2, H, both)
+    H[1, chunk(y, C)] = (up_slope * dgate + act * dup).astype(BF)
+    A[0, chunk(y, C)] = act.astype(BF)
+    A[1, chunk(y, C)] = up_slope.astype(BF)
+    half = C // 2
+
+    def piece(buf, n, q):
+        return lambda j: buf.at[n, pl.ds(pl.multiple_of(j * C + q * half, half), half)]
+
+    plans = [gather_ring(q, piece(H, n, q)) for n in (0, 1) for q in (0, 1)]
+    in_waves(plans)
     forward(4)
     forward(5)
     have(4)
     have(5)
-    finish(0)
+    plans[0][1]()
+    plans[1][1]()
     tangent = dot(H[0], W[5], 1, 1)
-    finish(1)
+    plans[2][1]()
+    plans[3][1]()
     tangent = tangent + dot(H[1], W[4], 1, 1)
 
     Tf[...] = tangent
     Tb[...] = tangent.astype(BF)
     tr = [send(Tb.at[chunk(up_t(r), R)], trecv.at[r - 1], tpeers[r - 1]) for r in range(1, NT)]
+    aplans = [gather_ring(n, lambda j, n=n: A.at[n, chunk(j, C)]) for n in (0, 1)]
+    aplans[0][0][1]()
+    aplans[1][0][1]()
     total = Tf[chunk(t, R)]
     for r in range(1, NT):
         tr[r - 1].arrive()
@@ -268,12 +357,14 @@
     tw = [send(wt.at[chunk(t, R)], wt.at[chunk(t, R)], p) for p in tpeers]
     osend[...] = total.astype(BF)
     oa = [send(osend, orecv.at[r - 1], ypeers[r - 1]) for r in range(1, NY)]
+    for w in range(2, NY // 2 + 1):
+        aplans[0][0][w]()
+        aplans[1][0][w]()
     for link in tw:
         link.arrive()
     weighted = wt[...]
 
     Pd[...] = dot(weighted, W[4], 1, 0)
-    half = C // 2
 
     def part_of(k, j):
         return Pd[pl.ds(pl.multiple_of(j * C + k * half, half), half)]
@@ -298,16 +389,16 @@
         stage2[i].arrive()
         out[...] = mine + zr[i].astype(F32)
 
-    def early():
+    plans = [reduce_tree(k, part_of, dh_s, dh_r) for k in (0, 1)]
+    in_waves(plans, None, {1: lambda: product(2, weighted, H[0])} if NY == 8 else None)
+    for k, (_, total) in enumerate(plans):
+        G[pl.ds(pl.multiple_of(y * C + k * half, half), half)] = total().astype(BF)
+    if NY != 8:
         product(2, weighted, H[0])
-
-    halves = reduce_scatter(
-        2, None, part_of, lambda k: part_of(k, y), dh_s, dh_r, both, (0, 0), {1: early}
-    )
-    dhid = jnp.concatenate(halves, axis=0)
-    B[0, chunk(y, C)] = (dhid * up * slope).astype(BF)
-    B[1, chunk(y, C)] = (dhid * act).astype(BF)
-    finish = all_gather(2, B, both)
+    plans = [gather_tree(k, lambda j, k=k: G.at[pl.ds(pl.multiple_of(j * C + k * half, half), half)]) for k in (0, 1)]
+    in_waves(plans)
+    for _, finish in aplans:
+        finish()
     cross(2)
 
     def two_rows(v):
@@ -325,10 +416,11 @@
             to[:, (zz * NY + j) * 2 * D : (zz * NY + j + 1) * 2 * D] = v[:, zz * 2 * D : (zz + 1) * 2 * D]
     settle(2, pd)
 
-    finish(0)
-    product(0, x, B[0])
-    finish(1)
-    product(1, x, B[1])
+    for _, finish in plans:
+        finish()
+    dhid = G[...].astype(F32)
+    product(0, x, (dhid * A[1].astype(F32)).astype(BF))
+    product(1, x, (dhid * A[0].astype(F32)).astype(BF))
     cross(0)
     cross(1)
     settle(0, pg)
@@ -343,8 +435,8 @@
     KP = -(-(K + 3) // 128) * 128
     R, C = 2 * NY, 2 * NT
     M = NT * R
-    long = NY // 2
-    n_links = 2 * (NY - 1) + 3 * (NT - 1) + 18 + 9 + 10 * (NY - 1)
+    steps = NY // 2
+    n_links = 2 * (NY - 1) + 3 * (NT - 1) + 18 + 9 + 14 * (NY - 1)
     vmem = pl.BlockSpec(memory_space=pltpu.VMEM)
     hbm = pl.BlockSpec(memory_space=pl.ANY)
     to, pg, pu, pd = pl.pallas_call(
@@ -364,12 +456,13 @@
             pltpu.VMEM((6, KP, F), BF),
             pltpu.VMEM((4, M, F), F32),
             pltpu.VMEM((M, F), F32),
-            pltpu.VMEM((4, 2, long, C, F), BF),
-            pltpu.VMEM((4, 2, long, C, F), BF),
-            pltpu.VMEM((2, 2, long, C // 2, F), BF),
-            pltpu.VMEM((2, 2, long, C // 2, F), BF),
+            pltpu.VMEM((4, 2, steps, C, F), BF),
+            pltpu.VMEM((4, 2, steps, C, F), BF),
+            pltpu.VMEM((2, 2, steps, C // 2, F), BF),
+            pltpu.VMEM((2, 2, steps, C // 2, F), BF),
             pltpu.VMEM((2, M, F), BF),
             pltpu.VMEM((2, M, F), BF),
+            pltpu.VMEM((M, F), BF),
             pltpu.VMEM((M, KP), F32),
             pltpu.VMEM((M, KP), BF),
             pltpu.VMEM((max(NT - 1, 1), R, KP), BF),

time: 137 us -> 131 us (0.956)
  Pallas kernels: 131 us -> 125 us
    pallas_call x1, Pallas kernels: 131 us -> 125 us  [on_device(): pl.pallas_call(functools.partial(kernel, NY, NT, D, F, KP), out_shape=[ja...]
where the time goes in v3:
time: 131 us; the launch traced here: 130 us
  Pallas kernels  125 us (95%)
  local copies, waits for them, and re-layouts  4.82 us (4%)
    pallas_call x1, Pallas kernels, on_device(): pl.pallas_call(functools.partial(kernel, NY, NT, D, F, KP), out_shape=[ja...  125 us
    unnamed x8, local copies, waits for them, and re-layouts  4.82 us

profile of v3, /device:TPU:1, one launch (start us, length us, event | category | flops | bytes accessed | tf_op | source)
XLA Modules:
  0.0 130.3 jit_solution(16151052020961419698)
XLA Ops:
  0.6 124.8 %shard_map.111 = (bf16[2,2560]{1,0:T(2,128)(2,1)}, f32[80,864]{1,0:T(8,128)}, f32[80,864]{1,0:T(8,128)}, f32[80,864]{1,0:T(8,128)}) custom-call(bf16[2,2560]{1,0:T(2,128)(2,1)} %x_in.1, f32[2]{0:T(128)} %curv_in.1, bf16[80,864]{1,0:T(8,128)(2,1)} %wg.1, bf16[80,864]{1,0:T(8,128)(2,1)} %wu.1, bf16[80,864]{1,0:T(8,128)(2,1)} %vg.1, bf16[80,864]{1,0:T(8,128)(2,1)} %vu.1, ...), custom_call_target="tpu_custom_call" | custom-call | tf_op jit(solution)/shard_map/pallas_call | solution.py:442
  125.4 1.3 %copy.16 = bf16[2,2560]{1,0:T(2,128)(2,1)} copy(bf16[2,2560]{1,0:T(2,128)(2,1)} %get-tuple-element.16) | data formatting | bytes 20480
  126.7 0.0 copy-start.1
  126.7 1.7 %copy.17 = f32[80,864]{1,0:T(8,128)} copy(f32[80,864]{1,0:T(8,128)} %get-tuple-element.17) | data formatting | bytes 552960
  128.5 0.0 copy-done.1
  128.5 0.0 copy-start
  128.5 0.7 copy.18
  129.2 0.3 copy-done
  129.5 0.7 copy.19
Async XLA Ops:
  126.7 1.7 %copy-start.1 = (f32[80,864]{1,0:T(8,128)S(1)}, f32[80,864]{1,0:T(8,128)}, u32[]{:S(2)}) copy-start(f32[80,864]{1,0:T(8,128)} %get-tuple-element.18) | copy-start | bytes 829444
  128.5 1.1 copy-start

commit v4 on v3

--- a/solution.py
+++ b/solution.py
@@ -297,8 +297,6 @@
     def begin(k):
         have(k)
         Pf[k] = dot(x, W[k], 1, 0)
-        if k in (1, 2):
-            forward(k + 1)
 
     plans = []
     for k in range(4):
@@ -311,11 +309,15 @@
         waves[1] = opened
         plans.append((waves, total))
 
+    def more():
+        forward(2)
+        forward(3)
+
     def down():
         fetch(4)
         fetch(5)
 
-    in_waves(plans, (0, 0, 1, 2), {2: down})
+    in_waves(plans, (0, 0, 1, 1), {1: more, 2: down} if NY == 8 else {1: lambda: (more(), down())})
     gate, up, dgate, dup = [total() for _, total in plans]
     sig = jax.nn.sigmoid(gate)
     act = gate * sig
@@ -346,7 +348,7 @@
     Tf[...] = tangent
     Tb[...] = tangent.astype(BF)
     tr = [send(Tb.at[chunk(up_t(r), R)], trecv.at[r - 1], tpeers[r - 1]) for r in range(1, NT)]
-    aplans = [gather_ring(n, lambda j, n=n: A.at[n, chunk(j, C)]) for n in (0, 1)]
+    aplans = [gather_tree(n, lambda j, n=n: A.at[n, chunk(j, C)]) for n in (0, 1)]
     aplans[0][0][1]()
     aplans[1][0][1]()
     total = Tf[chunk(t, R)]
@@ -357,7 +359,7 @@
     tw = [send(wt.at[chunk(t, R)], wt.at[chunk(t, R)], p) for p in tpeers]
     osend[...] = total.astype(BF)
     oa = [send(osend, orecv.at[r - 1], ypeers[r - 1]) for r in range(1, NY)]
-    for w in range(2, NY // 2 + 1):
+    for w in sorted(aplans[0][0])[1:]:
         aplans[0][0][w]()
         aplans[1][0][w]()
     for link in tw:
@@ -427,6 +429,11 @@
     settle(1, pu)
     for link in links:
         link.left()
+
+
+def hand_on(*refs):
+    for i in range(4):
+        refs[4 + i][...] = refs[i][...]
 
 
 def on_device(NY, NT, inputs, curvature, w_gate, w_up, w_down, v_gate, v_up, v_down):
@@ -483,6 +490,13 @@
             collective_id=0, has_side_effects=True, vmem_limit_bytes=62 * 1024 * 1024
         ),
     )(inputs, curvature, w_gate, w_up, v_gate, v_up, w_down.T, v_down.T)
+    arrays = (to, pg, pu, pd)
+    to, pg, pu, pd = pl.pallas_call(
+        hand_on,
+        out_shape=[jax.ShapeDtypeStruct(a.shape, a.dtype) for a in arrays],
+        in_specs=[vmem] * 4,
+        out_specs=[vmem] * 4,
+    )(*arrays)
     return to, pg, pu, pd.T
 
 

time: 131 us -> 122 us (0.931)
  local copies, waits for them, and re-layouts: 4.82 us -> 0 us
  Pallas kernels: 125 us -> 121 us
    pallas_call x1, Pallas kernels: 125 us -> 119 us  [on_device(): pl.pallas_call(functools.partial(kernel, NY, NT, D, F, KP), out_shape=[ja...]
    unnamed x8 -> x0, local copies, waits for them, and re-layouts: 4.82 us -> none
    pallas_call x0 -> x1, Pallas kernels: none -> 2.08 us  [on_device(): pl.pallas_call(hand_on, out_shape=[jax.ShapeDtypeStruct(a.shape, a.dtype)...]
where the time goes in v4:
time: 122 us; the launch traced here: 121 us
  Pallas kernels  121 us (99%)
    pallas_call x1, Pallas kernels, on_device(): pl.pallas_call(functools.partial(kernel, NY, NT, D, F, KP), out_shape=[ja...  119 us

profile of v4, /device:TPU:1, one launch (start us, length us, event | category | flops | bytes accessed | tf_op | source)
XLA Modules:
  0.0 121.4 jit_solution(9144019299696515927)
XLA Ops:
  0.6 118.7 %shard_map.111 = (bf16[2,2560]{1,0:T(2,128)(2,1)}, f32[80,864]{1,0:T(8,128)}, f32[80,864]{1,0:T(8,128)}, f32[80,864]{1,0:T(8,128)}) custom-call(bf16[2,2560]{1,0:T(2,128)(2,1)} %x_in.1, f32[2]{0:T(128)} %curv_in.1, bf16[80,864]{1,0:T(8,128)(2,1)} %wg.1, bf16[80,864]{1,0:T(8,128)(2,1)} %wu.1, bf16[80,864]{1,0:T(8,128)(2,1)} %vg.1, bf16[80,864]{1,0:T(8,128)(2,1)} %vu.1, ...), custom_call_target="tpu_custom_call" | custom-call | tf_op jit(solution)/shard_map/pallas_call | solution.py:449
  119.3 2.1 %shard_map.112 = (bf16[2,2560]{1,0:T(2,128)(2,1)}, f32[80,864]{1,0:T(8,128)}, f32[80,864]{1,0:T(8,128)}, f32[80,864]{1,0:T(8,128)}) custom-call(bf16[2,2560]{1,0:T(2,128)(2,1)} %get-tuple-element.12.refs_0_, f32[80,864]{1,0:T(8,128)} %get-tuple-element.13.refs_1_, f32[80,864]{1,0:T(8,128)} %get-tuple-element.14.refs_2_, f32[80,864]{1,0:T(8,128)} %get-tuple-element.15.refs_3_), custom_call_target="tpu_custom_call" | custom-call | tf_op jit(solution)/shard_map/pallas_call | solution.py:494

commit v5 on v4

--- a/solution.py
+++ b/solution.py
@@ -112,7 +112,8 @@
         stage[j] = jnp.where(lane == K + 1, mid, jnp.where(lane == K + 2, low, hi)).astype(BF)
     pl.semaphore_wait(barrier, len(peers))
 
-    xa = [send(stage.at[up_y(r)], xin.at[r - 1], ypeers[r - 1]) for r in range(1, NY)]
+    y_order = sorted(range(1, NY), key=lambda r: abs(r - NY // 2))
+    xa = {r - 1: send(stage.at[up_y(r)], xin.at[r - 1], ypeers[r - 1]) for r in y_order}
 
     own, other = z * 2 + c, (1 - z) * 2 + c
     mats = (wg, wu, vg, vu, wd, vd)
@@ -135,27 +136,28 @@
         forwards[k].arrive()
 
     fetch(0)
-    fetch(1)
     if KP > K:
         for k in range(6):
             W[k, K:KP, :] = jnp.zeros((KP - K, F), BF)
 
     x16 = stage[y].astype(F32)
-    for r in range(1, NY):
+    for r in reversed(y_order):
         xa[r - 1].arrive()
         x16 = x16 + xin[r - 1].astype(F32)
     curv = x16[:, K : K + 1] + x16[:, K + 1 : K + 2] + x16[:, K + 2 : K + 3]
     X[chunk(t, R)] = x16.astype(BF)
 
     def all_tensor(buf):
-        got = [send(buf.at[chunk(t, R)], buf.at[chunk(t, R)], p) for p in hpeers]
+        h_order = sorted(range(1, NH), key=lambda r: abs(r - NH // 2))
+        got = {r: send(buf.at[chunk(t, R)], buf.at[chunk(t, R)], hpeers[r - 1]) for r in h_order}
 
         def second():
             block = {}
             mine = [buf.at[chunk(t, R)]] + [buf.at[chunk(up_h(r), R)] for r in range(1, NH)]
-            for n, ref in enumerate(mine):
+            for n in [0] + h_order[::-1]:
+                ref = mine[n]
                 if n:
-                    got[NH - 1 - n].arrive()
+                    got[NH - n].arrive()
                 for p in xpeers:
                     block[n, len(block)] = send(ref, ref, p)
             return list(block.values())
@@ -163,8 +165,9 @@
         return second
 
     second = all_tensor(X)
+    fetch(1)
+    xg = second()
     fetch(2)
-    xg = second()
     fetch(3)
     forward(0)
     forward(1)
@@ -295,6 +298,8 @@
         return Pf[k, chunk(j, C)]
 
     def begin(k):
+        if k >= 2:
+            forward(k)
         have(k)
         Pf[k] = dot(x, W[k], 1, 0)
 
@@ -309,31 +314,41 @@
         waves[1] = opened
         plans.append((waves, total))
 
-    def more():
-        forward(2)
-        forward(3)
-
     def down():
         fetch(4)
         fetch(5)
 
-    in_waves(plans, (0, 0, 1, 1), {1: more, 2: down} if NY == 8 else {1: lambda: (more(), down())})
-    gate, up, dgate, dup = [total() for _, total in plans]
+    in_waves(plans, None, {1: down} if NY > 2 else None)
+    if NY == 2:
+        down()
+    half = C // 2
+
+    def piece(buf, n, q):
+        return lambda j: buf.at[n, pl.ds(pl.multiple_of(j * C + q * half, half), half)]
+
+    def steps_of(pair, w):
+        for waves, _ in pair:
+            if w in waves:
+                waves[w]()
+
+    gate, up = plans[0][1](), plans[1][1]()
     sig = jax.nn.sigmoid(gate)
     act = gate * sig
     slope = sig * (1.0 + gate * (1.0 - sig))
     up_slope = up * slope
     H[0, chunk(y, C)] = (act * up).astype(BF)
-    H[1, chunk(y, C)] = (up_slope * dgate + act * dup).astype(BF)
+    hid = [gather_tree(q, piece(H, 0, q)) for q in (0, 1)]
+    steps_of(hid, 1)
     A[0, chunk(y, C)] = act.astype(BF)
     A[1, chunk(y, C)] = up_slope.astype(BF)
-    half = C // 2
-
-    def piece(buf, n, q):
-        return lambda j: buf.at[n, pl.ds(pl.multiple_of(j * C + q * half, half), half)]
-
-    plans = [gather_ring(q, piece(H, n, q)) for n in (0, 1) for q in (0, 1)]
-    in_waves(plans)
+    dgate, dup = plans[2][1](), plans[3][1]()
+    H[1, chunk(y, C)] = (up_slope * dgate + act * dup).astype(BF)
+    thid = [gather_tree(q, piece(H, 1, q)) for q in (0, 1)]
+    steps_of(thid, 1)
+    for w in range(2, NY // 2 + 1):
+        steps_of(hid, w)
+        steps_of(thid, w)
+    plans = hid + thid
     forward(4)
     forward(5)
     have(4)
@@ -347,7 +362,8 @@
 
     Tf[...] = tangent
     Tb[...] = tangent.astype(BF)
-    tr = [send(Tb.at[chunk(up_t(r), R)], trecv.at[r - 1], tpeers[r - 1]) for r in range(1, NT)]
+    far_first = sorted(range(1, NT), key=lambda r: abs(r - NT // 2))
+    tr = {r - 1: send(Tb.at[chunk(up_t(r), R)], trecv.at[r - 1], tpeers[r - 1]) for r in far_first}
     aplans = [gather_tree(n, lambda j, n=n: A.at[n, chunk(j, C)]) for n in (0, 1)]
     aplans[0][0][1]()
     aplans[1][0][1]()
@@ -356,7 +372,7 @@
         tr[r - 1].arrive()
         total = total + trecv[r - 1].astype(F32)
     wt[chunk(t, R)] = (curv * total).astype(BF)
-    tw = [send(wt.at[chunk(t, R)], wt.at[chunk(t, R)], p) for p in tpeers]
+    tw = [send(wt.at[chunk(t, R)], wt.at[chunk(t, R)], tpeers[r - 1]) for r in far_first]
     osend[...] = total.astype(BF)
     oa = [send(osend, orecv.at[r - 1], ypeers[r - 1]) for r in range(1, NY)]
     for w in sorted(aplans[0][0])[1:]:
@@ -422,8 +438,9 @@
         finish()
     dhid = G[...].astype(F32)
     product(0, x, (dhid * A[1].astype(F32)).astype(BF))
-    product(1, x, (dhid * A[0].astype(F32)).astype(BF))
+    bup = (dhid * A[0].astype(F32)).astype(BF)
     cross(0)
+    product(1, x, bup)
     cross(1)
     settle(0, pg)
     settle(1, pu)

time: 122 us -> 116 us (0.951)
  Pallas kernels: 121 us -> 115 us
    pallas_call x1, Pallas kernels: 119 us -> 113 us  [on_device(): pl.pallas_call(functools.partial(kernel, NY, NT, D, F, KP), out_shape=[ja...]
where the time goes in v5:
time: 116 us
  Pallas kernels  115 us (99%)
    pallas_call x1, Pallas kernels, on_device(): pl.pallas_call(functools.partial(kernel, NY, NT, D, F, KP), out_shape=[ja...  113 us

profile of v5, /device:TPU:1, one launch (start us, length us, event | category | flops | bytes accessed | tf_op | source)
XLA Modules:
  0.0 115.8 jit_solution(17556327306693626406)
XLA Ops:
  0.6 113.1 %shard_map.111 = (bf16[2,2560]{1,0:T(2,128)(2,1)}, f32[80,864]{1,0:T(8,128)}, f32[80,864]{1,0:T(8,128)}, f32[80,864]{1,0:T(8,128)}) custom-call(bf16[2,2560]{1,0:T(2,128)(2,1)} %x_in.1, f32[2]{0:T(128)} %curv_in.1, bf16[80,864]{1,0:T(8,128)(2,1)} %wg.1, bf16[80,864]{1,0:T(8,128)(2,1)} %wu.1, bf16[80,864]{1,0:T(8,128)(2,1)} %vg.1, bf16[80,864]{1,0:T(8,128)(2,1)} %vu.1, ...), custom_call_target="tpu_custom_call" | custom-call | tf_op jit(solution)/shard_map/pallas_call | solution.py:466
  113.7 2.1 %shard_map.112 = (bf16[2,2560]{1,0:T(2,128)(2,1)}, f32[80,864]{1,0:T(8,128)}, f32[80,864]{1,0:T(8,128)}, f32[80,864]{1,0:T(8,128)}) custom-call(bf16[2,2560]{1,0:T(2,128)(2,1)} %get-tuple-element.12.refs_0_, f32[80,864]{1,0:T(8,128)} %get-tuple-element.13.refs_1_, f32[80,864]{1,0:T(8,128)} %get-tuple-element.14.refs_2_, f32[80,864]{1,0:T(8,128)} %get-tuple-element.15.refs_3_), custom_call_target="tpu_custom_call" | custom-call | tf_op jit(solution)/shard_map/pallas_call | solution.py:511

commit v6 on v5

--- a/solution.py
+++ b/solution.py
@@ -14,6 +14,10 @@
 
 def dot(a, b, ca, cb):
     return lax.dot_general(a, b, (((ca,), (cb,)), ((), ())), preferred_element_type=F32)
+
+
+def first_piece(F):
+    return (F // 2 + 127) // 128 * 128 if F > 256 else F // 2
 
 
 class Link:
@@ -39,8 +43,10 @@
     NY, NT, D, F, KP,
     x_in, curv_in, wg, wu, vg, vu, wd, vd,
     to, pg, pu, pd,
-    stage, xin, X, W, Pf, Pd, rs_s, rs_r, dh_s, dh_r, H, A, G,
-    Tf, Tb, trecv, wt, osend, orecv, ot, PF, PB, C1, zs, zr,
+    stage, xin, X, W, Pf, Pd, rs_s, rs_r, H, A,
+    Tf, Tb, trecv, wt, osend, orecv, ot, PF,
+    dh_sa, dh_ra, Ga, PBa, C1a, zsa, zra,
+    dh_sb, dh_rb, Gb, PBb, C1b, zsb, zrb,
     send_sems, recv_sems, local_sems,
 ):
     K = 4 * D
@@ -181,8 +187,9 @@
     def reach(k, d):
         return NY // 2 - (1 if (k % 2 == 0) == (d > 0) else 0)
 
-    def reduce_ring(k, part, sent, recv):
+    def reduce_ring(k, part, sent, recv, b=None):
         got = {}
+        b = k if b is None else b
 
         def step(s):
             for i, d in enumerate((-1, 1)):
@@ -192,26 +199,27 @@
                 v = part(k, up_y(d * (n - s + 1)))
                 if s > 1:
                     got[i].arrive()
-                    v = v + recv[k, i, s - 2].astype(F32)
-                sent[k, i, s - 1] = v.astype(BF)
-                got[i] = send(sent.at[k, i, s - 1], recv.at[k, i, s - 1], dist(d, 1))
+                    v = v + recv[b, i, s - 2].astype(F32)
+                sent[b, i, s - 1] = v.astype(BF)
+                got[i] = send(sent.at[b, i, s - 1], recv.at[b, i, s - 1], dist(d, 1))
 
         def total():
             v = part(k, y)
             for i, d in enumerate((-1, 1)):
                 if reach(k, d):
                     got[i].arrive()
-                    v = v + recv[k, i, reach(k, d) - 1].astype(F32)
+                    v = v + recv[b, i, reach(k, d) - 1].astype(F32)
             return v
 
         return {s: functools.partial(step, s) for s in range(1, NY // 2 + 1)}, total
 
-    def reduce_tree(k, part, sent, recv):
+    def reduce_tree(k, part, sent, recv, b=None):
         got = {}
+        b = k if b is None else b
 
         def push(i, d, slot, v, far):
-            sent[k, i, slot] = v.astype(BF)
-            got[i, slot] = send(sent.at[k, i, slot], recv.at[k, i, slot], dist(d, far))
+            sent[b, i, slot] = v.astype(BF)
+            got[i, slot] = send(sent.at[b, i, slot], recv.at[b, i, slot], dist(d, far))
 
         def first():
             for i, d in enumerate((-1, 1)):
@@ -226,7 +234,7 @@
                 v = part(k, up_y(2 * d))
                 for slot in (1, 0) if reach(k, d) == 4 else (1,):
                     got[i, slot].arrive()
-                    v = v + recv[k, i, slot].astype(F32)
+                    v = v + recv[b, i, slot].astype(F32)
                 push(i, d, 3, v, 2)
 
         def total():
@@ -234,7 +242,7 @@
             for slot in (2, 3):
                 for i in (0, 1):
                     got[i, slot].arrive()
-                    v = v + recv[k, i, slot].astype(F32)
+                    v = v + recv[b, i, slot].astype(F32)
             return v
 
         return {1: first, 2: second}, total
@@ -384,40 +392,49 @@
 
     Pd[...] = dot(weighted, W[4], 1, 0)
 
+    FA = first_piece(F)
+    lanes = (slice(0, FA), slice(FA, F))
+    dh_s, dh_r, G = (dh_sa, dh_sb), (dh_ra, dh_rb), (Ga, Gb)
+    PB, C1, zs, zr = (PBa, PBb), (C1a, C1b), (zsa, zsb), (zra, zrb)
+
+    stage1, stage2 = {}, {}
+
+    def product(i, q, lhs, rhs):
+        full = dot(lhs, rhs, 0, 0)
+        PF[i, :, lanes[q]] = full
+        PB[q][i] = full.astype(BF)
+        for n, zz in enumerate((1 - z, z)):
+            stage1[i, q, n] = send(PB[q].at[i, rows(zz * 2 + 1 - c)], C1[q].at[i, n], core)
+
+    def cross(i, q):
+        stage1[i, q, 0].arrive()
+        zs[q][i] = (PF[i, rows((1 - z) * 2 + c), lanes[q]] + C1[q][i, 0].astype(F32)).astype(BF)
+        stage2[i, q] = send(zs[q].at[i], zr[q].at[i], zed)
+
+    def settle(i, q, out):
+        stage1[i, q, 1].arrive()
+        mine = PF[i, rows(z * 2 + c), lanes[q]] + C1[q][i, 1].astype(F32)
+        stage2[i, q].arrive()
+        out[:, lanes[q]] = mine + zr[q][i].astype(F32)
+
     def part_of(k, j):
-        return Pd[pl.ds(pl.multiple_of(j * C + k * half, half), half)]
-
-    stage1, stage2 = {}, {}
-
-    def product(i, lhs, rhs):
-        full = dot(lhs, rhs, 0, 0)
-        PF[i] = full
-        PB[i] = full.astype(BF)
-        for n, zz in enumerate((1 - z, z)):
-            stage1[i, n] = send(PB.at[i, rows(zz * 2 + 1 - c)], C1.at[i, n], core)
-
-    def cross(i):
-        stage1[i, 0].arrive()
-        zs[i] = (PF[i, rows((1 - z) * 2 + c)] + C1[i, 0].astype(F32)).astype(BF)
-        stage2[i] = send(zs.at[i], zr.at[i], zed)
-
-    def settle(i, out):
-        stage1[i, 1].arrive()
-        mine = PF[i, rows(z * 2 + c)] + C1[i, 1].astype(F32)
-        stage2[i].arrive()
-        out[...] = mine + zr[i].astype(F32)
-
-    plans = [reduce_tree(k, part_of, dh_s, dh_r) for k in (0, 1)]
-    in_waves(plans, None, {1: lambda: product(2, weighted, H[0])} if NY == 8 else None)
-    for k, (_, total) in enumerate(plans):
-        G[pl.ds(pl.multiple_of(y * C + k * half, half), half)] = total().astype(BF)
-    if NY != 8:
-        product(2, weighted, H[0])
-    plans = [gather_tree(k, lambda j, k=k: G.at[pl.ds(pl.multiple_of(j * C + k * half, half), half)]) for k in (0, 1)]
-    in_waves(plans)
+        return Pd[chunk(j, C), lanes[k]]
+
+    sums = [reduce_tree(k, part_of, dh_s[k], dh_r[k], 0) for k in (0, 1)]
+    steps_of(sums, 1)
+    for q in (0, 1):
+        product(2, q, weighted, H[0, :, lanes[q]])
+    for w in range(2, NY // 2 + 1):
+        steps_of(sums, w)
+    back = []
+    for k in (0, 1):
+        G[k][chunk(y, C)] = sums[k][1]().astype(BF)
+        back.append(gather_tree(k, lambda j, k=k: G[k].at[chunk(j, C)]))
+        steps_of(back[k:], 1)
+    for q in (0, 1):
+        cross(2, q)
     for _, finish in aplans:
         finish()
-    cross(2)
 
     def two_rows(v):
         v = v.astype(F32)
@@ -428,22 +445,25 @@
             oa[r - 1].arrive()
         a, b = two_rows(orecv[r - 1] if r else osend[...])
         ot[up_y(-r)] = jnp.concatenate([a, b], axis=0)
+    for w in range(2, NY // 2 + 1):
+        steps_of(back, w)
     for j in range(NY):
         v = ot[j].astype(BF)
         for zz in (0, 1):
             to[:, (zz * NY + j) * 2 * D : (zz * NY + j + 1) * 2 * D] = v[:, zz * 2 * D : (zz + 1) * 2 * D]
-    settle(2, pd)
-
-    for _, finish in plans:
-        finish()
-    dhid = G[...].astype(F32)
-    product(0, x, (dhid * A[1].astype(F32)).astype(BF))
-    bup = (dhid * A[0].astype(F32)).astype(BF)
-    cross(0)
-    product(1, x, bup)
-    cross(1)
-    settle(0, pg)
-    settle(1, pu)
+
+    for q in (0, 1):
+        back[q][1]()
+        dhid = G[q][...].astype(F32)
+        product(0, q, x, (dhid * A[1, :, lanes[q]].astype(F32)).astype(BF))
+        bup = (dhid * A[0, :, lanes[q]].astype(F32)).astype(BF)
+        cross(0, q)
+        product(1, q, x, bup)
+        cross(1, q)
+    for q in (0, 1):
+        settle(2, q, pd)
+        settle(0, q, pg)
+        settle(1, q, pu)
     for link in links:
         link.left()
 
@@ -460,7 +480,20 @@
     R, C = 2 * NY, 2 * NT
     M = NT * R
     steps = NY // 2
-    n_links = 2 * (NY - 1) + 3 * (NT - 1) + 18 + 9 + 14 * (NY - 1)
+    FA = first_piece(F)
+
+    def piece(n):
+        return [
+            pltpu.VMEM((1, 2, steps, C, n), BF),
+            pltpu.VMEM((1, 2, steps, C, n), BF),
+            pltpu.VMEM((M, n), BF),
+            pltpu.VMEM((3, KP, n), BF),
+            pltpu.VMEM((3, 2, D, n), BF),
+            pltpu.VMEM((3, D, n), BF),
+            pltpu.VMEM((3, D, n), BF),
+        ]
+
+    n_links = 2 * (NY - 1) + 3 * (NT - 1) + 18 + 18 + 14 * (NY - 1)
     vmem = pl.BlockSpec(memory_space=pltpu.VMEM)
     hbm = pl.BlockSpec(memory_space=pl.ANY)
     to, pg, pu, pd = pl.pallas_call(
@@ -482,11 +515,8 @@
             pltpu.VMEM((M, F), F32),
             pltpu.VMEM((4, 2, steps, C, F), BF),
             pltpu.VMEM((4, 2, steps, C, F), BF),
-            pltpu.VMEM((2, 2, steps, C // 2, F), BF),
-            pltpu.VMEM((2, 2, steps, C // 2, F), BF),
             pltpu.VMEM((2, M, F), BF),
             pltpu.VMEM((2, M, F), BF),
-            pltpu.VMEM((M, F), BF),
             pltpu.VMEM((M, KP), F32),
             pltpu.VMEM((M, KP), BF),
             pltpu.VMEM((max(NT - 1, 1), R, KP), BF),
@@ -495,10 +525,8 @@
             pltpu.VMEM((NY - 1, R, KP), BF),
             pltpu.VMEM((NY, 2, KP), F32),
             pltpu.VMEM((3, KP, F), F32),
-            pltpu.VMEM((3, KP, F), BF),
-            pltpu.VMEM((3, 2, D, F), BF),
-            pltpu.VMEM((3, D, F), BF),
-            pltpu.VMEM((3, D, F), BF),
+            *piece(FA),
+            *piece(F - FA),
             pltpu.SemaphoreType.DMA((n_links,)),
             pltpu.SemaphoreType.DMA((n_links,)),
             pltpu.SemaphoreType.DMA((6,)),

time: 116 us -> 113 us (0.974)
  Pallas kernels: 115 us -> 113 us
    pallas_call x1, Pallas kernels: 113 us -> 111 us  [on_device(): pl.pallas_call(functools.partial(kernel, NY, NT, D, F, KP), out_shape=[ja...]
where the time goes in v6:
time: 113 us
  Pallas kernels  113 us (100%)
    pallas_call x1, Pallas kernels, on_device(): pl.pallas_call(functools.partial(kernel, NY, NT, D, F, KP), out_shape=[ja...  111 us

profile of v6, /device:TPU:1, one launch (start us, length us, event | category | flops | bytes accessed | tf_op | source)
XLA Modules:
  0.0 113.3 jit_solution(2697210438257343766)
XLA Ops:
  0.6 110.5 %shard_map.111 = (bf16[2,2560]{1,0:T(2,128)(2,1)}, f32[80,864]{1,0:T(8,128)}, f32[80,864]{1,0:T(8,128)}, f32[80,864]{1,0:T(8,128)}) custom-call(bf16[2,2560]{1,0:T(2,128)(2,1)} %x_in.1, f32[2]{0:T(128)} %curv_in.1, bf16[80,864]{1,0:T(8,128)(2,1)} %wg.1, bf16[80,864]{1,0:T(8,128)(2,1)} %wu.1, bf16[80,864]{1,0:T(8,128)(2,1)} %vg.1, bf16[80,864]{1,0:T(8,128)(2,1)} %vu.1, ...), custom_call_target="tpu_custom_call" | custom-call | tf_op jit(solution)/shard_map/pallas_call | solution.py:499
  111.2 2.1 %shard_map.112 = (bf16[2,2560]{1,0:T(2,128)(2,1)}, f32[80,864]{1,0:T(8,128)}, f32[80,864]{1,0:T(8,128)}, f32[80,864]{1,0:T(8,128)}) custom-call(bf16[2,2560]{1,0:T(2,128)(2,1)} %get-tuple-element.12.refs_0_, f32[80,864]{1,0:T(8,128)} %get-tuple-element.13.refs_1_, f32[80,864]{1,0:T(8,128)} %get-tuple-element.14.refs_2_, f32[80,864]{1,0:T(8,128)} %get-tuple-element.15.refs_3_), custom_call_target="tpu_custom_call" | custom-call | tf_op jit(solution)/shard_map/pallas_call | solution.py:539

commit v7 on v6

--- a/solution.py
+++ b/solution.py
@@ -103,19 +103,26 @@
     def chunk(j, size):
         return pl.ds(pl.multiple_of(j * size, size), size)
 
+    LT = KP // 128
     row = lax.broadcasted_iota(jnp.int32, (R, KP), 0)
-    lane = lax.broadcasted_iota(jnp.int32, (R, KP), 1)
+    lane = lax.broadcasted_iota(jnp.int32, (2, KP), 1)
+    packed = lax.broadcasted_iota(jnp.int32, (16, 128), 0)
+    placed = lax.broadcasted_iota(jnp.int32, (R, 128), 0)
     raw = x_in[...].astype(F32)
     tail = lax.broadcasted_iota(jnp.int32, (2, KP - K), 0)
     tail = jnp.where(tail == 0, curv_in[0], curv_in[1])
     for j in range(NY):
         parts = [raw[:, (zz * NY + j) * 2 * D : (zz * NY + j + 1) * 2 * D] for zz in (0, 1)]
         a = jnp.concatenate(parts + [tail], axis=1)
-        a = jnp.where(row == 2 * y, a[0:1], jnp.where(row == 2 * y + 1, a[1:2], 0.0))
         hi = a.astype(BF).astype(F32)
         mid = (a - hi).astype(BF).astype(F32)
         low = a - hi - mid
-        stage[j] = jnp.where(lane == K + 1, mid, jnp.where(lane == K + 2, low, hi)).astype(BF)
+        a = jnp.where(lane == K + 1, mid, jnp.where(lane == K + 2, low, hi))
+        block = jnp.zeros((16, 128), F32)
+        for i in (0, 1):
+            for m in range(LT):
+                block = jnp.where(packed == i * LT + m, a[i : i + 1, m * 128 : (m + 1) * 128], block)
+        stage[j] = block.astype(BF)
     pl.semaphore_wait(barrier, len(peers))
 
     y_order = sorted(range(1, NY), key=lambda r: abs(r - NY // 2))
@@ -146,10 +153,16 @@
         for k in range(6):
             W[k, K:KP, :] = jnp.zeros((KP - K, F), BF)
 
-    x16 = stage[y].astype(F32)
-    for r in reversed(y_order):
-        xa[r - 1].arrive()
-        x16 = x16 + xin[r - 1].astype(F32)
+    x16 = [jnp.zeros((R, 128), F32)] * LT
+    for r in [0] + y_order[::-1]:
+        if r:
+            xa[r - 1].arrive()
+        block = (xin[r - 1] if r else stage[y]).astype(F32)
+        for i in (0, 1):
+            here = placed == 2 * up_y(-r) + i
+            for m in range(LT):
+                x16[m] = jnp.where(here, block[i * LT + m : i * LT + m + 1], x16[m])
+    x16 = jnp.concatenate(x16, axis=1)
     curv = x16[:, K : K + 1] + x16[:, K + 1 : K + 2] + x16[:, K + 2 : K + 3]
     X[chunk(t, R)] = x16.astype(BF)
 
@@ -507,8 +520,8 @@
         in_specs=[vmem, pl.BlockSpec(memory_space=pltpu.SMEM)] + [hbm] * 6,
         out_specs=[vmem] * 4,
         scratch_shapes=[
-            pltpu.VMEM((NY, R, KP), BF),
-            pltpu.VMEM((NY - 1, R, KP), BF),
+            pltpu.VMEM((NY, 16, 128), BF),
+            pltpu.VMEM((NY - 1, 16, 128), BF),
             pltpu.VMEM((M, KP), BF),
             pltpu.VMEM((6, KP, F), BF),
             pltpu.VMEM((4, M, F), F32),

time: 113 us -> 113 us (level)
  no operation moved by 1% of the time
where the time goes in v7:
time: 113 us
  Pallas kernels  112 us (99%)
    pallas_call x1, Pallas kernels, on_device(): pl.pallas_call(functools.partial(kernel, NY, NT, D, F, KP), out_shape=[ja...  110 us

profile of v7, /device:TPU:1, one launch (start us, length us, event | category | flops | bytes accessed | tf_op | source)
XLA Modules:
  0.0 112.8 jit_solution(13318959887097748203)
XLA Ops:
  0.6 110.1 %shard_map.111 = (bf16[2,2560]{1,0:T(2,128)(2,1)}, f32[80,864]{1,0:T(8,128)}, f32[80,864]{1,0:T(8,128)}, f32[80,864]{1,0:T(8,128)}) custom-call(bf16[2,2560]{1,0:T(2,128)(2,1)} %x_in.1, f32[2]{0:T(128)} %curv_in.1, bf16[80,864]{1,0:T(8,128)(2,1)} %wg.1, bf16[80,864]{1,0:T(8,128)(2,1)} %wu.1, bf16[80,864]{1,0:T(8,128)(2,1)} %vg.1, bf16[80,864]{1,0:T(8,128)(2,1)} %vu.1, ...), custom_call_target="tpu_custom_call" | custom-call | tf_op jit(solution)/shard_map/pallas_call | solution.py:512
  110.7 2.1 %shard_map.112 = (bf16[2,2560]{1,0:T(2,128)(2,1)}, f32[80,864]{1,0:T(8,128)}, f32[80,864]{1,0:T(8,128)}, f32[80,864]{1,0:T(8,128)}) custom-call(bf16[2,2560]{1,0:T(2,128)(2,1)} %get-tuple-element.12.refs_0_, f32[80,864]{1,0:T(8,128)} %get-tuple-element.13.refs_1_, f32[80,864]{1,0:T(8,128)} %get-tuple-element.14.refs_2_, f32[80,864]{1,0:T(8,128)} %get-tuple-element.15.refs_3_), custom_call_target="tpu_custom_call" | custom-call | tf_op jit(solution)/shard_map/pallas_call | solution.py:552

commit v8 on v7

--- a/solution.py
+++ b/solution.py
@@ -17,7 +17,7 @@
 
 
 def first_piece(F):
-    return (F // 2 + 127) // 128 * 128 if F > 256 else F // 2
+    return F // 256 * 128 if F > 256 else F // 2
 
 
 class Link:
@@ -342,11 +342,6 @@
     in_waves(plans, None, {1: down} if NY > 2 else None)
     if NY == 2:
         down()
-    half = C // 2
-
-    def piece(buf, n, q):
-        return lambda j: buf.at[n, pl.ds(pl.multiple_of(j * C + q * half, half), half)]
-
     def steps_of(pair, w):
         for waves, _ in pair:
             if w in waves:
@@ -358,13 +353,13 @@
     slope = sig * (1.0 + gate * (1.0 - sig))
     up_slope = up * slope
     H[0, chunk(y, C)] = (act * up).astype(BF)
-    hid = [gather_tree(q, piece(H, 0, q)) for q in (0, 1)]
+    hid = [gather_tree(0, lambda j: H.at[0, chunk(j, C)])]
     steps_of(hid, 1)
     A[0, chunk(y, C)] = act.astype(BF)
     A[1, chunk(y, C)] = up_slope.astype(BF)
     dgate, dup = plans[2][1](), plans[3][1]()
     H[1, chunk(y, C)] = (up_slope * dgate + act * dup).astype(BF)
-    thid = [gather_tree(q, piece(H, 1, q)) for q in (0, 1)]
+    thid = [gather_tree(1, lambda j: H.at[1, chunk(j, C)])]
     steps_of(thid, 1)
     for w in range(2, NY // 2 + 1):
         steps_of(hid, w)
@@ -375,10 +370,8 @@
     have(4)
     have(5)
     plans[0][1]()
+    tangent = dot(H[0], W[5], 1, 1)
     plans[1][1]()
-    tangent = dot(H[0], W[5], 1, 1)
-    plans[2][1]()
-    plans[3][1]()
     tangent = tangent + dot(H[1], W[4], 1, 1)
 
     Tf[...] = tangent

time: 113 us -> 112 us (level)
  no operation moved by 1% of the time
where the time goes in v8:
time: 112 us
  Pallas kernels  112 us (100%)
    pallas_call x1, Pallas kernels, on_device(): pl.pallas_call(functools.partial(kernel, NY, NT, D, F, KP), out_shape=[ja...  109 us

profile of v8, /device:TPU:1, one launch (start us, length us, event | category | flops | bytes accessed | tf_op | source)
XLA Modules:
  0.0 112.2 jit_solution(14860077931181771111)
XLA Ops:
  0.6 109.5 %shard_map.111 = (bf16[2,2560]{1,0:T(2,128)(2,1)}, f32[80,864]{1,0:T(8,128)}, f32[80,864]{1,0:T(8,128)}, f32[80,864]{1,0:T(8,128)}) custom-call(bf16[2,2560]{1,0:T(2,128)(2,1)} %x_in.1, f32[2]{0:T(128)} %curv_in.1, bf16[80,864]{1,0:T(8,128)(2,1)} %wg.1, bf16[80,864]{1,0:T(8,128)(2,1)} %wu.1, bf16[80,864]{1,0:T(8,128)(2,1)} %vg.1, bf16[80,864]{1,0:T(8,128)(2,1)} %vu.1, ...), custom_call_target="tpu_custom_call" | custom-call | tf_op jit(solution)/shard_map/pallas_call | solution.py:505
  110.1 2.1 %shard_map.112 = (bf16[2,2560]{1,0:T(2,128)(2,1)}, f32[80,864]{1,0:T(8,128)}, f32[80,864]{1,0:T(8,128)}, f32[80,864]{1,0:T(8,128)}) custom-call(bf16[2,2560]{1,0:T(2,128)(2,1)} %get-tuple-element.12.refs_0_, f32[80,864]{1,0:T(8,128)} %get-tuple-element.13.refs_1_, f32[80,864]{1,0:T(8,128)} %get-tuple-element.14.refs_2_, f32[80,864]{1,0:T(8,128)} %get-tuple-element.15.refs_3_), custom_call_target="tpu_custom_call" | custom-call | tf_op jit(solution)/shard_map/pallas_call | solution.py:545
